TPU v7x, 128 devices: a whole 4x4x4 slice. The times are simulated.
128 devices in a mesh: lat: 8 (over y, z_hi), lon: 16 (over x, z_lo, core).
Axes of the slice: x: 4, y: 4, z: 4 (z_hi: 2, z_lo: 2; z = z_hi * 2 + z_lo), core: 2. Of those that a mesh axis runs over, the one named last changes fastest.
Arguments:
- tokens: bfloat16 [2, 96, 384, 512], P(None, 'lat', 'lon'), may hold values from -36 to 36
- cotangent: bfloat16 [2, 48, 192, 1024], P(None, 'lat', 'lon'), may hold values from -6 to 6
- gain_fine: float32 [512], replicated, may hold values from 0.25 to 1.75
- qkv_fine: bfloat16 [512, 1536], replicated, may hold values from -1.06066017 to 1.06066017
- proj_fine: bfloat16 [512, 512], replicated, may hold values from -0.25 to 0.25
- gain_merge: float32 [2048], replicated, may hold values from 0.25 to 1.75
- merge_weight: bfloat16 [2048, 1024], replicated, may hold values from -0.125 to 0.125
- gain_coarse: float32 [1024], replicated, may hold values from 0.25 to 1.75
- qkv_coarse: bfloat16 [1024, 3072], replicated, may hold values from -0.75 to 0.75
- proj_coarse: bfloat16 [1024, 1024], replicated, may hold values from -0.1875 to 0.1875
Outputs:
- coarse_tokens: bfloat16 [2, 48, 192, 1024], P(None, 'lat', 'lon')
- tokens_grad: bfloat16 [2, 96, 384, 512], P(None, 'lat', 'lon')
- gain_fine_grad: float32 [512], P(('lat', 'lon'))
- qkv_fine_grad: float32 [512, 1536], P(('lat', 'lon'))
- proj_fine_grad: float32 [512, 512], P(('lat', 'lon'))
- gain_merge_grad: float32 [2048], P(('lat', 'lon'))
- merge_grad: float32 [2048, 1024], P(('lat', 'lon'))
- gain_coarse_grad: float32 [1024], P(('lat', 'lon'))
- qkv_coarse_grad: float32 [1024, 3072], P(('lat', 'lon'))
- proj_coarse_grad: float32 [1024, 1024], P(('lat', 'lon'))
All inputs are finite; a program needn't handle non-finite values.
Results may differ from a plain program's by a relative error of at most 0.039.
Values may be sent and summed in bfloat16 or wider, within the bound.
A program may use at most 192 MiB of HBM per device.

v0:
```python
import jax
import jax.numpy as jnp
from jax import lax
from jax.sharding import PartitionSpec as P

HD = 64
WH = 6
WW = 12


EPSILON = 1e-05
MASKED = -1e30


def shifted(value, axis, steps):
    count = lax.axis_size(axis)
    pairs = [(source, (source + steps) % count) for source in range(count)]
    return lax.ppermute(value, axis, pairs)


def normalize(values, gain_vector):
    centre = jnp.mean(values, axis=-1, keepdims=True)
    offset = values - centre
    spread = jnp.mean(offset * offset, axis=-1, keepdims=True)
    return (offset * lax.rsqrt(spread + EPSILON) * gain_vector).astype(jnp.bfloat16)


def to_windows(block_grid, win_height, win_width):
    levels, row_count, col_count, features = block_grid.shape
    pieces = block_grid.reshape(
        levels, row_count // win_height, win_height, col_count // win_width, win_width, features
    )
    pieces = pieces.transpose(1, 3, 0, 2, 4, 5)
    return pieces.reshape(
        row_count // win_height * (col_count // win_width),
        levels * win_height * win_width,
        features,
    )


def from_windows(pieces, levels, row_count, col_count, win_height, win_width):
    features = pieces.shape[-1]
    grid_view = pieces.reshape(
        row_count // win_height, col_count // win_width, levels, win_height, win_width, features
    )
    grid_view = grid_view.transpose(2, 0, 3, 1, 4, 5)
    return grid_view.reshape(levels, row_count, col_count, features)


def visible(edge_flags, cell_count):
    places = jnp.arange(cell_count) // WW % WH
    upper_rows = places < WH - WH // 2
    same_group = upper_rows[:, None] == upper_rows[None, :]
    return jnp.logical_or(same_group[None, None], jnp.logical_not(edge_flags)[:, None, None, None])


def split_heads(windows, head_count):
    win_count, cell_count, triple_width = windows.shape
    features = triple_width // 3
    split_parts = windows.reshape(win_count, cell_count, 3, head_count, features // head_count)
    return (split_parts[:, :, 0], split_parts[:, :, 1], split_parts[:, :, 2])


def softmax_weights(queries, keys_part, edge_flags):
    score_scale = queries.shape[-1] ** (-0.5)
    scores = (
        jnp.einsum("wqhd,wkhd->whqk", queries, keys_part, preferred_element_type=jnp.float32)
        * score_scale
    )
    scores = jnp.where(visible(edge_flags, queries.shape[1]), scores, MASKED)
    highest = jnp.max(scores, axis=-1, keepdims=True)
    powers = jnp.exp(scores - highest)
    return powers / jnp.sum(powers, axis=-1, keepdims=True)


def attend(windows, edge_flags, head_count):
    queries, keys_part, values_part = split_heads(windows, head_count)
    weights = softmax_weights(queries, keys_part, edge_flags).astype(jnp.bfloat16)
    mixed_values = jnp.einsum(
        "whqk,wkhd->wqhd", weights, values_part, preferred_element_type=jnp.float32
    )
    return mixed_values.astype(jnp.bfloat16).reshape(windows.shape[0], windows.shape[1], -1)


def attend_back(windows, edge_flags, head_count, upstream):
    queries, keys_part, values_part = split_heads(windows, head_count)
    weights = softmax_weights(queries, keys_part, edge_flags)
    rounded = weights.astype(jnp.bfloat16)
    win_count, cell_count, features = upstream.shape
    incoming = upstream.reshape(win_count, cell_count, head_count, features // head_count)
    prob_grad = jnp.einsum(
        "wqhd,wkhd->whqk", incoming, values_part, preferred_element_type=jnp.float32
    )
    score_grad = weights * (prob_grad - jnp.sum(weights * prob_grad, axis=-1, keepdims=True))
    score_grad = (score_grad * queries.shape[-1] ** (-0.5)).astype(jnp.bfloat16)
    query_grad = jnp.einsum(
        "whqk,wkhd->wqhd", score_grad, keys_part, preferred_element_type=jnp.float32
    ).astype(jnp.bfloat16)
    key_grad = jnp.einsum(
        "whqk,wqhd->wkhd", score_grad, queries, preferred_element_type=jnp.float32
    ).astype(jnp.bfloat16)
    value_grad = jnp.einsum(
        "whqk,wqhd->wkhd", rounded, incoming, preferred_element_type=jnp.float32
    ).astype(jnp.bfloat16)
    return jnp.stack([query_grad, key_grad, value_grad], axis=2).reshape(
        win_count, cell_count, 3 * features
    )


def band_flags(win_count, row_count, col_count, last_band):
    band_index = jnp.arange(win_count) // (col_count // WW)
    return jnp.logical_and(band_index == row_count // WH - 1, last_band)


def attention_tile(qkv_tile, last_band, head_count):
    levels, row_count, col_count, triple_width = qkv_tile.shape
    windows = to_windows(qkv_tile, WH, WW)
    edge_flags = band_flags(windows.shape[0], row_count, col_count, last_band)
    return from_windows(
        attend(windows, edge_flags, head_count), levels, row_count, col_count, WH, WW
    )


def attention_tile_back(qkv_tile, last_band, head_count, upstream_tile):
    levels, row_count, col_count, triple_width = qkv_tile.shape
    windows = to_windows(qkv_tile, WH, WW)
    upstream = to_windows(upstream_tile, WH, WW)
    edge_flags = band_flags(windows.shape[0], row_count, col_count, last_band)
    return from_windows(
        attend_back(windows, edge_flags, head_count, upstream), levels, row_count, col_count, WH, WW
    )


def roll_ahead(grid_values):
    row_shift = WH // 2
    col_shift = WW // 2
    arrived = shifted(grid_values[:, :, :col_shift], "lon", -1)
    along_lon = jnp.concatenate([grid_values[:, :, col_shift:], arrived], axis=2)
    head_rows = along_lon[:, :row_shift]
    arrived_rows = shifted(head_rows, "lat", -1)
    return (jnp.concatenate([along_lon[:, row_shift:], arrived_rows], axis=1), along_lon)


def rows_behind(grid_values):
    row_shift = WH // 2
    row_count = grid_values.shape[1]
    tail_rows = grid_values[:, row_count - row_shift :]
    arrived = shifted(tail_rows, "lat", 1)
    return jnp.concatenate([arrived, grid_values[:, : row_count - row_shift]], axis=1)


def cols_behind(grid_values):
    col_shift = WW // 2
    col_count = grid_values.shape[2]
    arrived = shifted(grid_values[:, :, col_count - col_shift :], "lon", 1)
    return jnp.concatenate([arrived, grid_values[:, :, : col_count - col_shift]], axis=2)


def as_rows(grid_values):
    return grid_values.reshape(-1, grid_values.shape[-1])


def weight_gradient(left_grid, right_grid):
    return jnp.dot(as_rows(left_grid).T, as_rows(right_grid), preferred_element_type=jnp.float32)


def merge_patches(grid_values):
    levels, row_count, col_count, features = grid_values.shape
    pieces = grid_values.reshape(levels, row_count // 2, 2, col_count // 2, 2, features)
    return pieces.transpose(0, 1, 3, 4, 2, 5).reshape(
        levels, row_count // 2, col_count // 2, 4 * features
    )


def split_patches(grid_values):
    levels, row_count, col_count, features = grid_values.shape
    pieces = grid_values.reshape(levels, row_count, col_count, 2, 2, features // 4)
    return pieces.transpose(0, 1, 4, 2, 3, 5).reshape(
        levels, 2 * row_count, 2 * col_count, features // 4
    )


def level_forward(tokens_f, gain_vector, qkv_weight, proj_weight):
    head_count = qkv_weight.shape[0] // HD
    last_band = lax.axis_index("lat") == lax.axis_size("lat") - 1
    normed = normalize(tokens_f, gain_vector)
    rolled, along_lon = roll_ahead(normed)
    qkv_tile = jnp.dot(rolled, qkv_weight, preferred_element_type=jnp.float32).astype(jnp.bfloat16)
    attended = rows_behind(attention_tile(qkv_tile, last_band, head_count))
    edge_tile = None
    edge_qkv = None
    attended = cols_behind(attended)
    output = (tokens_f + jnp.dot(attended, proj_weight, preferred_element_type=jnp.float32)).astype(
        jnp.bfloat16
    )
    return (output, (rolled, qkv_tile, attended, edge_tile, edge_qkv))


def level_backward(tokens_f, gain_vector, qkv_weight, proj_weight, saved, result_grad):
    rolled, qkv_tile, attended, edge_tile, edge_qkv = saved
    head_count = qkv_weight.shape[0] // HD
    last_band = lax.axis_index("lat") == lax.axis_size("lat") - 1
    proj_grad = weight_gradient(attended, result_grad)
    attended_grad = jnp.dot(result_grad, proj_weight.T, preferred_element_type=jnp.float32).astype(
        jnp.bfloat16
    )
    rolled_attn_grad, along_grad = roll_ahead(attended_grad)
    qkv_grad = attention_tile_back(qkv_tile, last_band, head_count, rolled_attn_grad)
    qkv_weight_grad = weight_gradient(rolled, qkv_grad)
    rolled_grad = jnp.dot(qkv_grad, qkv_weight.T, preferred_element_type=jnp.float32).astype(
        jnp.bfloat16
    )
    normed_grad = rows_behind(rolled_grad)
    normed_grad = cols_behind(normed_grad)
    normed_value, pullback = jax.vjp(normalize, tokens_f, gain_vector)
    tokens_ln_grad, gain_grad = pullback(normed_grad)
    return (result_grad.astype(jnp.float32) + tokens_ln_grad, gain_grad, qkv_weight_grad, proj_grad)


def local(
    tokens,
    cotangent,
    gain_fine,
    qkv_fine,
    proj_fine,
    gain_merge,
    merge_weight,
    gain_coarse,
    qkv_coarse,
    proj_coarse,
):
    tokens_f = tokens.astype(jnp.float32)
    fine_out, fine_saved = level_forward(tokens_f, gain_fine, qkv_fine, proj_fine)
    patches = merge_patches(fine_out).astype(jnp.float32)
    merged_norm = normalize(patches, gain_merge)
    coarse_in = jnp.dot(merged_norm, merge_weight, preferred_element_type=jnp.float32).astype(
        jnp.bfloat16
    )
    coarse_f = coarse_in.astype(jnp.float32)
    coarse_tokens, coarse_saved = level_forward(coarse_f, gain_coarse, qkv_coarse, proj_coarse)
    coarse_grad_f, gain_coarse_grad, qkv_coarse_grad, proj_coarse_grad = level_backward(
        coarse_f, gain_coarse, qkv_coarse, proj_coarse, coarse_saved, cotangent
    )
    coarse_grad = coarse_grad_f.astype(jnp.bfloat16)
    merge_grad = weight_gradient(merged_norm, coarse_grad)
    merged_norm_grad = jnp.dot(
        coarse_grad, merge_weight.T, preferred_element_type=jnp.float32
    ).astype(jnp.bfloat16)
    normed_value, pullback = jax.vjp(normalize, patches, gain_merge)
    patches_grad, gain_merge_grad = pullback(merged_norm_grad)
    fine_grad = split_patches(patches_grad).astype(jnp.bfloat16)
    tokens_grad_f, gain_fine_grad, qkv_fine_grad, proj_fine_grad = level_backward(
        tokens_f, gain_fine, qkv_fine, proj_fine, fine_saved, fine_grad
    )
    shares = tuple(
        (
            lax.psum_scatter(gain_fine_grad, ("lat", "lon"), scatter_dimension=0, tiled=True),
            lax.psum_scatter(qkv_fine_grad, ("lat", "lon"), scatter_dimension=0, tiled=True),
            lax.psum_scatter(proj_fine_grad, ("lat", "lon"), scatter_dimension=0, tiled=True),
            lax.psum_scatter(gain_merge_grad, ("lat", "lon"), scatter_dimension=0, tiled=True),
            lax.psum_scatter(merge_grad, ("lat", "lon"), scatter_dimension=0, tiled=True),
            lax.psum_scatter(gain_coarse_grad, ("lat", "lon"), scatter_dimension=0, tiled=True),
            lax.psum_scatter(qkv_coarse_grad, ("lat", "lon"), scatter_dimension=0, tiled=True),
            lax.psum_scatter(proj_coarse_grad, ("lat", "lon"), scatter_dimension=0, tiled=True),
        )
    )
    return (coarse_tokens, tokens_grad_f.astype(jnp.bfloat16)) + shares


def solution(mesh):
    placed = (
        P(None, "lat", "lon", None),
        P(None, "lat", "lon", None),
        P(),
        P(),
        P(),
        P(),
        P(),
        P(),
        P(),
        P(),
    )
    return jax.shard_map(
        local,
        mesh=mesh,
        in_specs=placed,
        out_specs=(
            P(None, "lat", "lon", None),
            P(None, "lat", "lon", None),
            P(("lat", "lon")),
            P(("lat", "lon"), None),
            P(("lat", "lon"), None),
            P(("lat", "lon")),
            P(("lat", "lon"), None),
            P(("lat", "lon")),
            P(("lat", "lon"), None),
            P(("lat", "lon"), None),
        ),
        check_vma=False,
    )
```

profile of v0, /device:TPU:0, one launch (start us, length us, event | category | flops | bytes accessed | tf_op | source)
XLA Modules:
  0.0 2397.3 jit_solution(3437197812730675489)
XLA Ops:
  19.2 6.1 collective-permute-start.1
  33.7 6.8 reshape_reshape.16
  40.5 4.1 fusion.205
  69.2 5.6 collective-permute-done.2
  96.8 4.1 fusion.212
  103.3 3.9 collective-permute-start.9
  117.9 5.4 fusion.13
  139.9 4.2 fusion.213
  147.2 5.6 fusion.111
  152.8 5.6 fusion.114
  161.3 4.1 copy.220
  169.2 5.4 fusion.106
  175.6 9.7 collective-permute-done.10
  185.9 7.2 collective-permute-done.11
  228.6 4.7 fusion.76
  236.3 9.4 fusion.69
  245.8 9.4 fusion.72
  255.2 4.3 pad_maximum_fusion
  259.5 6.7 copy.238
  266.1 6.7 reshape_reshape.19
  280.0 4.8 fusion.218
  293.9 9.9 collective-permute-done.6
  304.0 8.1 collective-permute-done.7
  316.5 6.5 convolution_bitcast_fusion
  326.6 8.0 fusion.219
  341.8 7.9 collective-permute-done.14
  352.6 5.6 collective-permute-done.15
  361.6 62.9 %all-reduce.5 = (f32[512]{0:T(512)S(1)}, f32[2048]{0:T(1024)S(1)}, f32[1024]{0:T(1024)S(1)}) all-reduce(f32[512]{0:T(512)S(1)} %get-tuple-element.62, f32[2048]{0:T(1024)S(1)} %copy-done.42, f32[1024]{0:T(1024)S(1)} %copy-done.44), channel_id=2, replica_groups=mesh['lat'=8,'lon'=16] {'lat','lon'}, use_global_device_ids=true, to_apply=%region_19.20.clone | all-reduce | flops 3584 | bytes 28672
  428.8 14.3 all-reduce.9.cloned.1.call-done
  445.9 643.1 %reduce-scatter.8.cloned.1.call-done = f32[8,1024]{1,0:T(8,128)} async-done(((f32[1024,1024]{1,0:T(8,128)}), f32[8,1024]{1,0:T(8,128)}) %reduce-scatter.8.cloned.1.call-update) | async-done | bytes 32784 | tf_op jit(solution)/shard_map/reduce_scatter | solution.py:264
  1088.9 647.0 %reduce-scatter.4.cloned.1.call-done = f32[16,1024]{1,0:T(8,128)} async-done(((f32[2048,1024]{1,0:T(8,128)}), f32[16,1024]{1,0:T(8,128)}) %reduce-scatter.4.cloned.1.call-update) | async-done | bytes 65552 | tf_op jit(solution)/shard_map/reduce_scatter | solution.py:261
  1735.9 654.4 %reduce-scatter.6.cloned.1.call-done = f32[8,3072]{1,0:T(8,128)} async-done(((f32[1024,3072]{1,0:T(8,128)}), f32[8,3072]{1,0:T(8,128)}) %reduce-scatter.6.cloned.1.call-update) | async-done | bytes 98320 | tf_op jit(solution)/shard_map/reduce_scatter | solution.py:263
  (250 shorter events, 190.8 us)
Async XLA Ops:
  7.2 60.9 %copy-start = (bf16[1024,1024]{1,0:T(8,128)(2,1)S(1)}, bf16[1024,1024]{1,0:T(8,128)(2,1)}, u32[]{:S(2)}) copy-start(bf16[1024,1024]{1,0:T(8,128)(2,1)} %param.19) | copy-start | bytes 6291460
  7.2 436.0 %all-reduce.9.cloned.1.call-start = ((), (), s32[]{:S(2)}) async-start(), calls=%async_computation.6 | async-start | bytes 8388608
  12.0 7.1 collective-permute-start
  16.4 11.6 copy-start.45
  19.2 8.8 collective-permute-start.1
  65.4 9.5 collective-permute-start.2
  68.9 13.3 copy-start.1
  68.9 13.3 copy-start.11
  74.9 7.3 collective-permute-start.3
  75.9 26.3 %collective-permute-start.8 = (bf16[2,6,6,1024]{3,2,1,0:T(8,128)(2,1)}, bf16[2,6,6,1024]{3,2,1,0:T(8,128)(2,1)}, u32[]{:S(2)}, u32[]{:S(2)}) collective-permute-start(bf16[2,6,6,1024]{3,2,1,0:T(8,128)(2,1)} %get-tuple-element.82), channel_id=1, source_target_pairs={{0,15},{1,0},{2,1},{3,2},{4,3},{5,4},{6,5},{7,6},{8,7},{9,8},{10,9... | collective-permute-start | bytes 442376 | tf_op jit(solution)/shard_map/ppermute | solution.py:18
  102.1 5.1 collective-permute-start.4
  103.3 9.2 collective-permute-start.9
  108.1 9.7 collective-permute-start.5
  169.2 23.8 copy-start.39
  174.6 18.8 copy-start.37
  174.6 19.9 copy-start.18
  174.7 10.6 collective-permute-start.10
  185.4 7.7 collective-permute-start.11
  210.5 3.3 collective-permute-start.12
  213.8 6.9 collective-permute-start.13
  284.8 804.1 %reduce-scatter.8.cloned.1.call-start = ((), (), s32[]{:S(2)}) async-start(), calls=%async_computation.5 | async-start | bytes 4227072 | tf_op jit(solution)/shard_map/reduce_scatter | solution.py:264
  293.8 18.3 copy-start.15
  293.8 10.0 collective-permute-start.6
  303.9 8.1 collective-permute-start.7
  316.4 1419.5 %reduce-scatter.4.cloned.1.call-start = ((), (), s32[]{:S(2)}) async-start(), calls=%async_computation.3 | async-start | bytes 8454144 | tf_op jit(solution)/shard_map/reduce_scatter | solution.py:261
  323.0 2067.3 %reduce-scatter.6.cloned.1.call-start = ((), (), s32[]{:S(2)}) async-start(), calls=%async_computation.4 | async-start | bytes 12681216 | tf_op jit(solution)/shard_map/reduce_scatter | solution.py:263
  340.7 9.1 collective-permute-start.14
  340.7 10.3 copy-start.24
  340.7 10.3 copy-start.29
  341.8 18.0 copy-start.4
  350.6 7.6 collective-permute-start.15
  351.6 74.6 %copy-start.6 = (bf16[2,12,24,512]{3,2,1,0:T(8,128)(2,1)S(1)}, bf16[2,12,24,512]{3,2,1,0:T(8,128)(2,1)}, u32[]{:S(2)}) copy-start(bf16[2,12,24,512]{3,2,1,0:T(8,128)(2,1)} %convert_element_type.214) | copy-start | bytes 1769476
  (37 other events, 160.2 us)
Sparse Core Ops, SparseCore 0:
  284.9 158.1 all-reduce.8
  446.1 642.8 reduce-scatter.7
  1092.0 643.8 reduce-scatter.3
  1738.8 651.4 reduce-scatter.5
where the time goes:
time: 2410 us; the launch traced here: 2400 us
  waiting for transfers between devices  2030 us (84%)
  local copies, waits for them, and re-layouts  127 us (5%)
  matrix products  104 us (4%)
  blocking collectives  62.9 us (3%)
  other arithmetic  35.1 us (1%)
  starting transfers between devices  28.2 us (1%)
    reduce_scatter x1, waiting for transfers between devices, local(): lax.psum_scatter(qkv_coarse_grad, ('lat', 'lon'), scatter_dimension=0, ti...  654 us
    reduce_scatter x1, waiting for transfers between devices, local(): lax.psum_scatter(merge_grad, ('lat', 'lon'), scatter_dimension=0, tiled=T...  647 us
    reduce_scatter x1, waiting for transfers between devices, local(): lax.psum_scatter(proj_coarse_grad, ('lat', 'lon'), scatter_dimension=0, t...  643 us
    ppermute x16, waiting for transfers between devices, shifted(): return lax.ppermute(value, axis, pairs)  67 us
    unnamed x1, blocking collectives  62.9 us
  transfers between devices with their start and end apart: 20, of which 17 were waited for; matrix products, arithmetic and copies ran while one was open for 3% of the time, Pallas kernels for 0%

commit v1 on v0

v1 whole, which is shorter than its diff:
```python
import functools

import jax
import jax.numpy as jnp
import numpy as np
from jax import lax
from jax.experimental import pallas as pl
from jax.experimental.pallas import tpu as pltpu
from jax.sharding import PartitionSpec as P

MESH = pl.DeviceIdType.MESH
HALF = jnp.bfloat16
FULL = jnp.float32
HD = 64
WH = 6
WW = 12
CELLS = 144
EPSILON = 1e-05
MASKED = -1e30
LIMIT = 58 * 1024 * 1024
VMEM = pl.BlockSpec(memory_space=pltpu.VMEM)
SMEM = pl.BlockSpec(memory_space=pltpu.SMEM)
ANYWHERE = pl.BlockSpec(memory_space=pl.ANY)


def dot(left, right):
    return jnp.dot(left, right, preferred_element_type=FULL)


def dot_nt(left, right):
    return lax.dot_general(left, right, (((1,), (1,)), ((), ())), preferred_element_type=FULL)


def dot_tn(left, right):
    return lax.dot_general(left, right, (((0,), (0,)), ((), ())), preferred_element_type=FULL)


def natural_order(rows, cols):
    return lambda level, i, j: (level * rows + i) * cols + j


def window_order(rows, cols):
    def place(level, i, j):
        window = i // WH * (cols // WW) + j // WW
        return window * CELLS + ((i % WH // 3 * 2 + level) * 3 + i % 3) * WW + j % WW

    return place


def patch_order(rows, cols):
    coarse = window_order(rows // 2, cols // 2)

    def place(level, i, j):
        return (j % 2 * 2 + i % 2) * CELLS + coarse(level, i // 2, j // 2)

    return place


@functools.lru_cache(maxsize=None)
def roll_matrices(rows, cols, source, target, sign):
    orders = {"natural": natural_order, "window": window_order, "patch": patch_order}
    from_place, to_place = orders[source](rows, cols), orders[target](rows, cols)
    count = 2 * rows * cols
    pieces = ([], [], [])
    own = np.zeros((count, count), np.float32)
    for level in range(2):
        for i in range(rows):
            for j in range(cols):
                far_i, far_j = i + 3 * sign, j + 6 * sign
                across = (far_i // rows != 0, far_j // cols != 0)
                here = from_place(level, far_i % rows, far_j % cols)
                there = to_place(level, i, j)
                if across == (False, False):
                    own[there, here] = 1
                else:
                    slot = {(False, True): 0, (True, False): 1, (True, True): 2}[across]
                    pieces[slot].append((there, here))
    sizes = tuple((len(piece) + 15) // 16 * 16 for piece in pieces)
    pack = np.zeros((sum(sizes), count), np.float32)
    halo = np.zeros((count, sum(sizes)), np.float32)
    start = 0
    for piece, size in zip(pieces, sizes):
        for k, (there, here) in enumerate(piece):
            pack[start + k, here] = 1
            halo[there, start + k] = 1
        start += size
    return pack, own, halo, sizes


def roll_kernel(count, sizes, sign, *refs):
    given = [refs[4 * n : 4 * n + 4] for n in range(count)]
    result = refs[4 * count : 5 * count]
    packed = refs[5 * count : 6 * count]
    landed = refs[6 * count : 7 * count]
    send_sem, recv_sem = refs[7 * count :]
    lat, lon = lax.axis_index("lat"), lax.axis_index("lon")
    lats, lons = lax.axis_size("lat"), lax.axis_size("lon")
    steps = ((0, 1), (1, 0), (1, 1))

    def neighbour(step, way):
        return (
            lax.rem(lat + lats + way * step[0], lats),
            lax.rem(lon + lons + way * step[1], lons),
        )

    barrier = pltpu.get_barrier_semaphore()
    for step in steps:
        pl.semaphore_signal(
            barrier, inc=1, device_id=neighbour(step, sign), device_id_type=MESH
        )
    for n in range(count):
        value, pack, own, halo = given[n]
        packed[n][...] = dot(pack[...], value[...]).astype(HALF)
    pl.semaphore_wait(barrier, 3)
    copies = []
    for n in range(count):
        start = 0
        for slot, step in enumerate(steps):
            rows = pl.ds(start, sizes[n][slot])
            copy = pltpu.make_async_remote_copy(
                src_ref=packed[n].at[rows],
                dst_ref=landed[n].at[rows],
                send_sem=send_sem.at[n, slot],
                recv_sem=recv_sem.at[n, slot],
                device_id=neighbour(step, -sign),
                device_id_type=MESH,
            )
            copy.start()
            copies.append(copy)
            start += sizes[n][slot]
    for n in range(count):
        value, pack, own, halo = given[n]
        result[n][...] = dot(own[...], value[...]).astype(HALF)
    for n in range(count):
        value, pack, own, halo = given[n]
        for copy in copies[3 * n : 3 * n + 3]:
            copy.wait()
        result[n][...] = result[n][...] + dot(halo[...], landed[n][...]).astype(HALF)


def roll_grids(items, sign, identity):
    count = len(items)
    operands, shapes, packed, landed, sizes = [], [], [], [], []
    for value, rows, cols, source, target in items:
        pack, own, halo, size = roll_matrices(rows, cols, source, target, sign)
        operands += [value] + [jnp.asarray(matrix, HALF) for matrix in (pack, own, halo)]
        shapes.append(jax.ShapeDtypeStruct(value.shape, HALF))
        packed.append(pltpu.VMEM((sum(size), value.shape[1]), HALF))
        landed.append(pltpu.VMEM((sum(size), value.shape[1]), HALF))
        sizes.append(size)
    return pl.pallas_call(
        functools.partial(roll_kernel, count, tuple(sizes), sign),
        out_shape=shapes,
        in_specs=[VMEM] * len(operands),
        out_specs=[VMEM] * count,
        scratch_shapes=packed
        + landed
        + [pltpu.SemaphoreType.DMA((count, 3)), pltpu.SemaphoreType.DMA((count, 3))],
        compiler_params=pltpu.CompilerParams(
            collective_id=identity, has_side_effects=True, vmem_limit_bytes=LIMIT
        ),
    )(*operands)


def norm_parts(values):
    centre = jnp.mean(values, axis=-1, keepdims=True)
    offset = values - centre
    spread = jnp.mean(offset * offset, axis=-1, keepdims=True)
    scale = lax.rsqrt(spread + EPSILON)
    return offset * scale, scale


def norm_back(grad, normal, scale, gain):
    inner = grad * gain
    mean = jnp.mean(inner, axis=-1, keepdims=True)
    along = jnp.mean(inner * normal, axis=-1, keepdims=True)
    return (inner - mean - normal * along) * scale


def two_heads(pair):
    first = lax.broadcasted_iota(jnp.int32, pair.shape, 1) < HD
    zero = jnp.zeros_like(pair)
    return jnp.concatenate([jnp.where(first, pair, zero), jnp.where(first, zero, pair)], axis=0)


def one_pair(stack):
    half = stack.shape[0] // 2
    first = lax.broadcasted_iota(jnp.int32, (half, 2 * HD), 1) < HD
    return jnp.where(first, stack[:half], stack[half:])


def pair_mask(edge):
    shape = (CELLS, 2 * CELLS)
    key = lax.broadcasted_iota(jnp.int32, shape, 0)
    query = lax.broadcasted_iota(jnp.int32, shape, 1)
    query = jnp.where(query >= CELLS, query - CELLS, query)
    apart = (key < CELLS // 2) != (query < CELLS // 2)
    return jnp.where(apart, edge, 0) > 0


def pair_weights(queries, keys, mask):
    scores = dot_nt(keys, queries * 0.125)
    scores = jnp.where(mask, MASKED, scores)
    powers = jnp.exp(scores - jnp.max(scores, axis=0, keepdims=True))
    return powers * (1.0 / jnp.sum(powers, axis=0, keepdims=True))


def pair_forward(weights, values):
    return one_pair(dot_tn(weights.astype(HALF), values)).astype(HALF)


def pair_back(weights, queries, keys, values, upstream):
    weight_grad = dot_nt(values, upstream)
    inner = jnp.sum(weights * weight_grad, axis=0, keepdims=True)
    score_grad = (weights * (weight_grad - inner) * 0.125).astype(HALF)
    query_grad = one_pair(dot_tn(score_grad, keys)).astype(HALF)
    key_grad = dot(score_grad, queries).astype(HALF)
    value_grad = dot(weights.astype(HALF), upstream).astype(HALF)
    return query_grad, key_grad, value_grad


def fine_forward_kernel(edge, tokens, gain, qkv_w, proj_w, normal, qkv, attended, result):
    def window(w, carry):
        rows = pl.ds(pl.multiple_of(w * CELLS, 16), CELLS)
        values = tokens[rows, :].astype(FULL)
        unit, _ = norm_parts(values)
        normed = (unit * gain[...]).astype(HALF)
        normal[rows, :] = normed
        qkv[rows, :] = dot(normed, qkv_w[...]).astype(HALF)
        mask = pair_mask(jnp.where(w >= 2, edge[0], 0))
        for p in range(4):
            at = 128 * p
            queries = two_heads(qkv[rows, at : at + 128])
            weights = pair_weights(queries, qkv[rows, 512 + at : 640 + at], mask)
            attended[rows, at : at + 128] = pair_forward(weights, qkv[rows, 1024 + at : 1152 + at])
        result[rows, :] = (values + dot(attended[rows, :], proj_w[...])).astype(HALF)
        return carry

    lax.fori_loop(0, 4, window, 0)


def fine_forward(edge, tokens, gain, qkv_w, proj_w):
    return pl.pallas_call(
        fine_forward_kernel,
        out_shape=[jax.ShapeDtypeStruct((576, width), HALF) for width in (512, 1536, 512, 512)],
        in_specs=[SMEM] + [VMEM] * 4,
        out_specs=[VMEM] * 4,
        compiler_params=pltpu.CompilerParams(vmem_limit_bytes=LIMIT),
    )(edge, tokens, gain, qkv_w, proj_w)


def coarse_kernel(
    edge,
    patches,
    cotangent,
    gain_merge,
    gain_coarse,
    merge_any,
    qkv_any,
    proj_any,
    tokens_out,
    patches_grad,
    share_a,
    share_b,
    share_c,
    merge_w,
    qkv_w,
    proj_w,
    unit_merge,
    merged,
    unit_coarse,
    normed,
    qkv,
    attended,
    attended_grad,
    qkv_grad,
    inner_grad,
    weights_all,
    sems,
):
    loads = [
        pltpu.make_async_copy(source, target, sems.at[n])
        for n, (source, target) in enumerate(
            ((merge_any, merge_w), (proj_any, proj_w), (qkv_any, qkv_w))
        )
    ]
    for load in loads:
        load.start()
    values = jnp.concatenate(
        [patches[CELLS * g : CELLS * (g + 1), :] for g in range(4)], axis=1
    ).astype(FULL)
    unit, scale_merge = norm_parts(values)
    unit_merge[...] = unit
    merged[...] = (unit * gain_merge[...]).astype(HALF)
    loads[0].wait()
    coarse_in = dot(merged[...], merge_w[...]).astype(HALF).astype(FULL)
    unit, scale_coarse = norm_parts(coarse_in)
    unit_coarse[...] = unit
    normed[...] = (unit * gain_coarse[...]).astype(HALF)
    loads[1].wait()
    attended_grad[...] = dot_nt(cotangent[...], proj_w[...]).astype(HALF)
    loads[2].wait()
    for n in range(3):
        cols = slice(1024 * n, 1024 * (n + 1))
        qkv[:, cols] = dot(normed[...], qkv_w[:, cols]).astype(HALF)
    mask = pair_mask(edge[0])
    for p in range(8):
        at = 128 * p
        queries = two_heads(qkv[:, at : at + 128])
        weights = pair_weights(queries, qkv[:, 1024 + at : 1152 + at], mask)
        attended[:, at : at + 128] = pair_forward(weights, qkv[:, 2048 + at : 2176 + at])
        upstream = two_heads(attended_grad[:, at : at + 128])
        grads = pair_back(
            weights, queries, qkv[:, 1024 + at : 1152 + at], qkv[:, 2048 + at : 2176 + at], upstream
        )
        for n in range(3):
            qkv_grad[:, 1024 * n + at : 1024 * n + at + 128] = grads[n]
    tokens_out[...] = (coarse_in + dot(attended[...], proj_w[...])).astype(HALF)
    normed_grad = dot_nt(qkv_grad[...], qkv_w[...]).astype(HALF).astype(FULL)
    gain_coarse_terms = (normed_grad * unit_coarse[...]).astype(HALF)
    coarse_grad = cotangent[...].astype(FULL) + norm_back(
        normed_grad, unit_coarse[...], scale_coarse, gain_coarse[...]
    )
    inner_grad[...] = coarse_grad.astype(HALF)
    merged_grad = dot_nt(inner_grad[...], merge_w[...]).astype(HALF).astype(FULL)
    gain_merge_terms = (merged_grad * unit_merge[...]).astype(HALF)
    back = norm_back(merged_grad, unit_merge[...], scale_merge, gain_merge[...]).astype(HALF)
    for g in range(4):
        patches_grad[CELLS * g : CELLS * (g + 1), :] = back[:, 512 * g : 512 * (g + 1)]
    ones = jnp.ones((CELLS, 128), HALF)
    left_lane = lax.broadcasted_iota(jnp.int32, (128, 16, 128), 2) < HD
    by_merge = dot_tn(gain_merge_terms, ones).reshape(128, 16, 128)
    by_coarse = dot_tn(gain_coarse_terms, ones).reshape(128, 8, 128)
    by_coarse = jnp.concatenate([by_coarse, by_coarse], axis=1)
    share_a[:, :, 1024:] = jnp.where(left_lane, by_merge, by_coarse).astype(HALF)

    def merge_rows(n, carry):
        left = merged[:, pl.ds(pl.multiple_of(n * 256, 256), 256)]
        grad = dot_tn(left, inner_grad[...])
        share_a[pl.ds(n * 16, 16), :, :1024] = grad.reshape(16, 16, 1024).astype(HALF)
        return carry

    lax.fori_loop(0, 8, merge_rows, 0)

    def paired(grad, low, high):
        width = low.stop - low.start
        pieces = [grad[:, part].reshape(32, 8, width) for part in (low, high)]
        return jnp.concatenate(pieces, axis=1).astype(HALF)

    def other_rows(n, carry):
        cols = pl.ds(pl.multiple_of(n * 256, 256), 256)
        owners = pl.ds(n * 32, 32)
        left = normed[:, cols]
        for low, high, share, at in (
            (0, 1536, share_b, 0),
            (512, 2048, share_b, 512),
            (1024, 2560, share_c, 0),
        ):
            right = jnp.concatenate(
                [qkv_grad[:, low : low + 512], qkv_grad[:, high : high + 512]], axis=1
            )
            grad = dot_tn(left, right)
            share[owners, :, at : at + 512] = paired(grad, slice(0, 512), slice(512, 1024))
        grad = dot_tn(attended[:, cols], cotangent[...])
        share_c[owners, :, 512:] = paired(grad, slice(0, 512), slice(512, 1024))
        return carry

    lax.fori_loop(0, 4, other_rows, 0)


def coarse_level(edge, patches, cotangent, gain_merge, gain_coarse, merge_w, qkv_w, proj_w):
    half = lambda *shape: pltpu.VMEM(shape, HALF)
    full = lambda *shape: pltpu.VMEM(shape, FULL)
    return pl.pallas_call(
        coarse_kernel,
        out_shape=[
            jax.ShapeDtypeStruct((CELLS, 1024), HALF),
            jax.ShapeDtypeStruct((576, 512), HALF),
            jax.ShapeDtypeStruct((128, 16, 1152), HALF),
            jax.ShapeDtypeStruct((128, 16, 1024), HALF),
            jax.ShapeDtypeStruct((128, 16, 1024), HALF),
        ],
        in_specs=[SMEM] + [VMEM] * 4 + [ANYWHERE] * 3,
        out_specs=[VMEM] * 5,
        scratch_shapes=[
            half(2048, 1024),
            half(1024, 3072),
            half(1024, 1024),
            full(CELLS, 2048),
            half(CELLS, 2048),
            full(CELLS, 1024),
            half(CELLS, 1024),
            half(CELLS, 3072),
            half(CELLS, 1024),
            half(CELLS, 1024),
            half(CELLS, 3072),
            half(CELLS, 1024),
            full(8, 128),
            pltpu.SemaphoreType.DMA((3,)),
        ],
        compiler_params=pltpu.CompilerParams(vmem_limit_bytes=LIMIT),
    )(edge, patches, cotangent, gain_merge, gain_coarse, merge_w, qkv_w, proj_w)


def four_stacked(pieces):
    rows, width = pieces[0].shape
    shaped = [piece.reshape(rows // 8, 8, width) for piece in pieces]
    upper = lax.broadcasted_iota(jnp.int32, shaped[0].shape, 1) < 4
    turned = [pltpu.roll(piece, 4, 1) for piece in shaped]
    even = [jnp.where(upper, shaped[n], turned[n + 1]) for n in (0, 2)]
    odd = [jnp.where(upper, turned[n], shaped[n + 1]) for n in (0, 2)]
    return [jnp.concatenate(pair, axis=1).astype(HALF) for pair in (even, odd)]


def fine_backward_kernel(
    edge,
    tokens,
    normal,
    qkv,
    attended,
    result_grad,
    gain,
    qkv_w,
    proj_w,
    tokens_grad,
    share_a,
    share_b,
    share_c,
    qkv_grad,
    terms,
):
    def window(w, carry):
        rows = pl.ds(pl.multiple_of(w * CELLS, 16), CELLS)
        attended_grad = dot_nt(result_grad[rows, :], proj_w[...]).astype(HALF)
        mask = pair_mask(jnp.where(w >= 2, edge[0], 0))
        for p in range(4):
            at = 128 * p
            queries = two_heads(qkv[rows, at : at + 128])
            keys = qkv[rows, 512 + at : 640 + at]
            weights = pair_weights(queries, keys, mask)
            grads = pair_back(
                weights,
                queries,
                keys,
                qkv[rows, 1024 + at : 1152 + at],
                two_heads(attended_grad[:, at : at + 128]),
            )
            for n in range(3):
                qkv_grad[rows, 512 * n + at : 512 * n + at + 128] = grads[n]
        normed_grad = dot_nt(qkv_grad[rows, :], qkv_w[...]).astype(HALF).astype(FULL)
        unit, scale = norm_parts(tokens[rows, :].astype(FULL))
        terms[rows, :] = (normed_grad * unit).astype(HALF)
        back = norm_back(normed_grad, unit, scale, gain[...])
        tokens_grad[rows, :] = (result_grad[rows, :].astype(FULL) + back).astype(HALF)
        return carry

    lax.fori_loop(0, 4, window, 0)
    ones = jnp.ones((576, 128), HALF)

    def weight_rows(n, carry):
        cols = pl.ds(pl.multiple_of(n * 128, 128), 128)
        owners = pl.ds(n * 16, 16)

        def store(share, at, pieces):
            width = pieces[0].shape[1]
            for side, value in enumerate(four_stacked(pieces)):
                share[owners, side, :, at : at + width] = value

        grad = dot_tn(normal[:, cols], qkv_grad[...])
        store(share_a, 0, [grad[:, 384 * m : 384 * m + 256] for m in range(4)])
        store(share_b, 0, [grad[:, 384 * m + 256 : 384 * m + 384] for m in range(4)])
        grad = dot_tn(attended[:, cols], result_grad[...])
        store(share_b, 128, [grad[:, 128 * m : 128 * m + 128] for m in range(4)])
        store(share_c, 0, [dot_tn(terms[:, cols], ones)] * 4)
        return carry

    lax.fori_loop(0, 4, weight_rows, 0)


def fine_backward(edge, tokens, normal, qkv, attended, result_grad, gain, qkv_w, proj_w):
    return pl.pallas_call(
        fine_backward_kernel,
        out_shape=[jax.ShapeDtypeStruct((576, 512), HALF)]
        + [jax.ShapeDtypeStruct((64, 2, 16, width), HALF) for width in (256, 256, 128)],
        in_specs=[SMEM] + [VMEM] * 8,
        out_specs=[VMEM] * 4,
        scratch_shapes=[pltpu.VMEM((576, 1536), HALF), pltpu.VMEM((576, 512), HALF)],
        compiler_params=pltpu.CompilerParams(vmem_limit_bytes=LIMIT),
    )(edge, tokens, normal, qkv, attended, result_grad, gain, qkv_w, proj_w)


def device_parts(
    tokens,
    cotangent,
    gain_fine,
    qkv_fine,
    proj_fine,
    gain_merge,
    merge_weight,
    gain_coarse,
    qkv_coarse,
    proj_coarse,
):
    last = lax.axis_index("lat") == lax.axis_size("lat") - 1
    edge = last.astype(jnp.int32).reshape(1)
    gain_f = gain_fine.reshape(1, 512)
    gain_m = gain_merge.reshape(1, 2048)
    gain_c = gain_coarse.reshape(1, 1024)
    rolled, cotangent_rolled = roll_grids(
        [
            (tokens.reshape(576, 512), 12, 24, "natural", "window"),
            (cotangent.reshape(CELLS, 1024), 6, 12, "natural", "window"),
        ],
        1,
        1,
    )
    normal, qkv, attended, fine_out = fine_forward(edge, rolled, gain_f, qkv_fine, proj_fine)
    (patches,) = roll_grids([(fine_out, 12, 24, "window", "patch")], 1, 2)
    coarse_out, patches_grad, *coarse_shares = coarse_level(
        edge, patches, cotangent_rolled, gain_m, gain_c, merge_weight, qkv_coarse, proj_coarse
    )
    coarse_tokens, fine_grad = roll_grids(
        [
            (coarse_out, 6, 12, "window", "natural"),
            (patches_grad, 12, 24, "patch", "window"),
        ],
        -1,
        3,
    )
    tokens_grad, *fine_shares = fine_backward(
        edge, rolled, normal, qkv, attended, fine_grad, gain_f, qkv_fine, proj_fine
    )
    (tokens_grad,) = roll_grids([(tokens_grad, 12, 24, "window", "natural")], -1, 4)
    return (
        coarse_tokens.reshape(2, 6, 12, 1024),
        tokens_grad.reshape(2, 12, 24, 512),
        coarse_shares,
        fine_shares,
    )


ORDERS = (("x", "y", "z"), ("y", "z", "x"), ("z", "x", "y"))
LEADS = (((4, 2, 2), (2, 2)), ((2, 4, 2), (4,)), ((4, 4), (4,)))


def position():
    lat = lax.axis_index("lat")
    lon = lax.axis_index("lon")
    return {"y": lat // 2, "x": lon // 4, "z": lat % 2 * 2 + lon // 2 % 2}, lon % 2


def device_at(place, core):
    lat = place["y"] * 2 + place["z"] // 2
    lon = place["x"] * 4 + place["z"] % 2 * 2 + core
    return (lat, lon)


def along(place, axis, steps):
    moved = dict(place)
    moved[axis] = lax.rem(place[axis] + steps, 4)
    return moved


def first_cut(kind, ref, index, core):
    if kind == 0:
        return ref.at[:, :, index, :, core]
    if kind == 1:
        return ref.at[index, :, :, :, core]
    return ref.at[:, index // 2, :, index % 2, core]


def second_cut(kind, ref, index):
    if kind == 0:
        return ref.at[index]
    if kind == 1:
        return ref.at[index // 2, :, index % 2]
    return ref.at[:, index]


def third_cut(kind, ref, index):
    if kind == 0:
        return ref.at[index // 2, index % 2]
    return ref.at[index]


def spots(lead, i):
    found = []
    for size in reversed(lead):
        found.insert(0, i % size)
        i = i // size
    return tuple(found)


def greet(place, core):
    barrier = pltpu.get_barrier_semaphore()
    partners = [device_at(place, 1 - core)] + [
        device_at(along(place, axis, k), core) for axis in ("x", "y", "z") for k in (1, 2, 3)
    ]
    for partner in partners:
        pl.semaphore_signal(barrier, inc=1, device_id=partner, device_id_type=MESH)
    pl.semaphore_wait(barrier, len(partners))


def scatter_steps(place, core, given, own, first, landed, summed, sems):
    local_sem, send_sem, recv_sem = sems
    parts = range(len(given))
    sibling = device_at(place, 1 - core)

    def remote(source, target, p, slot, device):
        return pltpu.make_async_remote_copy(
            src_ref=source,
            dst_ref=target,
            send_sem=send_sem.at[p, slot],
            recv_sem=recv_sem.at[p, slot],
            device_id=device,
            device_id_type=MESH,
        )

    pairs, keeps = {}, {}
    for k in (1, 2, 3, 0):
        for p in parts:
            index = lax.rem(place[ORDERS[p % 3][0]] + k, 4)
            pairs[p, k] = remote(
                first_cut(p % 3, given[p], index, 1 - core), first[p].at[k], p, k, sibling
            )
            pairs[p, k].start()
            keeps[p, k] = pltpu.make_async_copy(
                first_cut(p % 3, given[p], index, core), own[p].at[k], local_sem.at[p, k]
            )
            keeps[p, k].start()

    sends = {}
    for k in (1, 2, 3, 0):
        for p in parts:
            pairs[p, k].wait()
            keeps[p, k].wait()

            def add_one(i, carry, p=p, k=k):
                at = (k,) + spots(LEADS[p % 3][0], i)
                first[p][at] = first[p][at] + own[p][at]
                return carry

            lax.fori_loop(0, 16, add_one, 0)
            if k > 0:
                target = device_at(along(place, ORDERS[p % 3][0], k), core)
                sends[p, k] = remote(first[p].at[k], landed[p][0].at[k - 1], p, 3 + k, target)
                sends[p, k].start()

    def added(base, arrivals):
        total = base.astype(FULL)
        for arrival in arrivals:
            total = total + arrival.astype(FULL)
        return total

    second = {}
    for p in parts:
        for k in (1, 2, 3):
            sends[p, k].wait()

        def add_three(i, carry, p=p):
            at = spots(LEADS[p % 3][0], i)
            total = added(first[p][(0,) + at], [landed[p][0][(k,) + at] for k in range(3)])
            summed[p][0][at] = total.astype(HALF)
            return carry

        lax.fori_loop(0, 16, add_three, 0)
        axis = ORDERS[p % 3][1]
        for k in (1, 2, 3):
            moved = along(place, axis, k)
            second[p, k] = remote(
                second_cut(p % 3, summed[p][0], moved[axis]),
                landed[p][1].at[k - 1],
                p,
                6 + k,
                device_at(moved, core),
            )
            second[p, k].start()
    third = {}
    for p in parts:
        for k in (1, 2, 3):
            second[p, k].wait()
        mine = second_cut(p % 3, summed[p][0], place[ORDERS[p % 3][1]])
        total = added(mine[...], [landed[p][1][k] for k in range(3)])
        summed[p][1][...] = total.astype(HALF)
        axis = ORDERS[p % 3][2]
        for k in (1, 2, 3):
            moved = along(place, axis, k)
            third[p, k] = remote(
                third_cut(p % 3, summed[p][1], moved[axis]),
                landed[p][2].at[k - 1],
                p,
                9 + k,
                device_at(moved, core),
            )
            third[p, k].start()
    results = []
    for p in parts:
        for k in (1, 2, 3):
            third[p, k].wait()
        mine = third_cut(p % 3, summed[p][1], place[ORDERS[p % 3][2]])
        results.append(added(mine[...], [landed[p][2][k] for k in range(3)]))
    return results


def scatter_scratch(widths):
    scratch = []
    for n, width in enumerate(widths):
        lead = LEADS[n % 3]
        scratch += [
            pltpu.VMEM((4,) + lead[0] + (16, width), HALF),
            pltpu.VMEM((4,) + lead[0] + (16, width), HALF),
            pltpu.VMEM((3,) + lead[0] + (16, width), HALF),
            pltpu.VMEM((3,) + lead[1] + (16, width), HALF),
            pltpu.VMEM((3, 16, width), HALF),
            pltpu.VMEM(lead[0] + (16, width), HALF),
            pltpu.VMEM(lead[1] + (16, width), HALF),
        ]
    count = len(widths)
    return scratch + [
        pltpu.SemaphoreType.DMA((count, 4)),
        pltpu.SemaphoreType.DMA((count, 13)),
        pltpu.SemaphoreType.DMA((count, 13)),
    ]


def scatter_groups(scratch, count):
    groups = [scratch[7 * p : 7 * p + 7] for p in range(count)]
    return (
        [group[0] for group in groups],
        [group[1] for group in groups],
        [group[2:5] for group in groups],
        [group[5:7] for group in groups],
        scratch[7 * count :],
    )


def write_coarse(shares, merge_out, qkv_out, proj_out, gains_out):
    a, b, c = shares
    merge_out[...] = a[:, :1024]
    gains_out[...] = a[:, 1024:]
    for n in range(2):
        rows = slice(8 * n, 8 * n + 8)
        qkv_out[:, 1536 * n : 1536 * n + 1024] = b[rows]
        qkv_out[:, 1536 * n + 1024 : 1536 * n + 1536] = c[rows, :512]
        proj_out[:, 512 * n : 512 * n + 512] = c[rows, 512:]


def write_fine(shares, qkv_out, proj_out, gains_out):
    a, b, c = shares
    gains_out[...] = c
    for n in range(4):
        rows = slice(4 * n, 4 * n + 4)
        qkv_out[:, 384 * n : 384 * n + 256] = a[rows]
        qkv_out[:, 384 * n + 256 : 384 * n + 384] = b[rows, :128]
        proj_out[:, 128 * n : 128 * n + 128] = b[rows, 128:]


COARSE_OUT = ((16, 1024), (8, 3072), (8, 1024), (16, 128))
FINE_OUT = ((4, 1536), (4, 512), (16, 128))


def scatter_kernel(*refs):
    given, outs, scratch = refs[:6], refs[6:13], refs[13:]
    place, core = position()
    greet(place, core)
    results = scatter_steps(place, core, given, *scatter_groups(scratch, 6))
    write_coarse(results[:3], *outs[:4])
    write_fine(results[3:], *outs[4:])


def scatter_sum(arrays, identity):
    arrays = [array.reshape(4, 2, 4, 2, 2, 16, array.shape[-1]) for array in arrays]
    widths = [array.shape[-1] for array in arrays]
    return pl.pallas_call(
        scatter_kernel,
        out_shape=[jax.ShapeDtypeStruct(shape, FULL) for shape in COARSE_OUT + FINE_OUT],
        in_specs=[ANYWHERE] * 6,
        out_specs=[VMEM] * 7,
        scratch_shapes=scatter_scratch(widths),
        compiler_params=pltpu.CompilerParams(
            collective_id=identity, has_side_effects=True, vmem_limit_bytes=LIMIT
        ),
    )(*arrays)


def local(*args):
    coarse_tokens, tokens_grad, coarse_shares, fine_shares = device_parts(*args)
    merge, qkv_c, proj_c, gains_c, qkv_f, proj_f, gains_f = scatter_sum(
        list(coarse_shares) + list(fine_shares), 5
    )
    return (
        coarse_tokens,
        tokens_grad,
        gains_f[:4, 0],
        qkv_f,
        proj_f,
        gains_c[:, 0],
        merge,
        gains_c[:8, HD],
        qkv_c,
        proj_c,
    )


def solution(mesh):
    grid = P(None, "lat", "lon", None)
    vector, matrix = P(("lat", "lon")), P(("lat", "lon"), None)
    return jax.shard_map(
        local,
        mesh=mesh,
        in_specs=(grid, grid) + (P(),) * 8,
        out_specs=(grid, grid, vector, matrix, matrix, vector, matrix, vector, matrix, matrix),
        check_vma=False,
    )
```

time: 2410 us -> 186 us (0.08)
  waiting for transfers between devices: 2030 us -> 0 us
  Pallas kernels: 0 us -> 170 us
  local copies, waits for them, and re-layouts: 127 us -> 14.7 us
  matrix products: 104 us -> 0 us
  blocking collectives: 62.9 us -> 0 us
  other arithmetic: 35.1 us -> 0 us
  starting transfers between devices: 28.2 us -> 0 us
    reduce_scatter x3 -> x0, waiting for transfers between devices: 1940 us -> none  [the longest x1 654 us: local(): lax.psum_scatter(qkv_coarse_grad, ('lat', 'lon'), scatter_dimension=0, ti...]
    pallas_call x0 -> x8, Pallas kernels: none -> 170 us  [the longest x4 63.6 us: roll_grids(): pl.pallas_call(functools.partial(roll_kernel, count, tuple(sizes), sign),...]
    dot_general x26 -> x0, matrix products: 99.5 us -> none  [the longest x5 24.5 us: weight_gradient(): jnp.dot(as_rows(left_grid).T, as_rows(right_grid), preferred_element_type...]
    ppermute x16 -> x0, waiting for transfers between devices: 67 us -> none  [shifted(): return lax.ppermute(value, axis, pairs)]
    unnamed x1 -> x0, blocking collectives: 62.9 us -> none
    another operation x13 -> x0, local copies, waits for them, and re-layouts: 49.7 us -> none  [the longest x2 10.8 us: attend_back(): jnp.stack([query_grad, key_grad, value_grad], axis=2)]
    ppermute x16 -> x0, starting transfers between devices: 27.8 us -> none  [shifted(): return lax.ppermute(value, axis, pairs)]
  transfers between devices with their start and end apart: 20 -> 0, of which waited for: 17 -> 0; matrix products, arithmetic and copies ran while one was open for 3% -> 0% of each run, Pallas kernels for 0% -> 0%
where the time goes in v1:
time: 186 us
  Pallas kernels  170 us (91%)
  local copies, waits for them, and re-layouts  14.7 us (8%)
    pallas_call x4, Pallas kernels, roll_grids(): pl.pallas_call(functools.partial(roll_kernel, count, tuple(sizes), sign),...  63.6 us
    pallas_call x1, Pallas kernels, scatter_sum(): pl.pallas_call(scatter_kernel, out_shape=[jax.ShapeDtypeStruct(shape, FUL...  55.7 us
    pallas_call x1, Pallas kernels, coarse_level(): pl.pallas_call(coarse_kernel, out_shape=[jax.ShapeDtypeStruct((CELLS, 102...  25.5 us
    pallas_call x1, Pallas kernels, fine_backward(): pl.pallas_call(fine_backward_kernel, out_shape=[jax.ShapeDtypeStruct((576...  17.5 us
    unnamed x12, local copies, waits for them, and re-layouts  9.9 us
    pallas_call x1, Pallas kernels, fine_forward(): pl.pallas_call(fine_forward_kernel, out_shape=[jax.ShapeDtypeStruct((576,...  7.99 us

profile of v1, /device:TPU:0, one launch (start us, length us, event | category | flops | bytes accessed | tf_op | source)
XLA Modules:
  0.0 185.7 jit_solution(17954590596333215699)
XLA Ops:
  0.6 1.0 copy.40
  1.7 0.8 reshape.67.refs_4_
  2.5 17.9 %shard_map.339 = (bf16[576,512]{1,0:T(8,128)(2,1)}, bf16[144,1024]{1,0:T(8,128)(2,1)}) custom-call(bf16[576,512]{1,0:T(8,128)(2,1)} %bitcast.18, bf16[272,576]{1,0:T(8,128)(2,1)} %constant.44.clone.refs_1_, bf16[576,576]{1,0:T(8,128)(2,1)} %constant.45.clone.refs_2_, bf16[576,272]{1,0:T(8,128)(2,1)} %constant.46.clone.refs_3_, ...), custom_call_target="tpu_custom_call" | custom-call | tf_op jit(solution)/shard_map/pallas_call | solution.py:151
  20.4 8.0 %shard_map.340 = (bf16[576,512]{1,0:T(8,128)(2,1)}, bf16[576,1536]{1,0:T(8,128)(2,1)}, bf16[576,512]{1,0:T(8,128)(2,1)}, bf16[576,512]{1,0:T(8,128)(2,1)}) custom-call(s32[1]{0:T(128)} %bitcast.edge, bf16[576,512]{1,0:T(8,128)(2,1)} %get-tuple-element.34.tokens, f32[1,512]{1,0:T(1,128)} %bitcast.20, bf16[512,1536]{1,0:T(8,128)(2,1)} %qkv_w.3, ...), custom_call_target="tpu_custom_call" | custom-call | tf_op jit(solution)/shard_map/pallas_call | solution.py:243
  28.4 13.4 %shard_map.341.patches = bf16[576,512]{1,0:T(8,128)(2,1)} custom-call(bf16[576,512]{1,0:T(8,128)(2,1)} %get-tuple-element.35.refs_0_, bf16[272,576]{1,0:T(8,128)(2,1)} %constant.50.clone.refs_1_, bf16[576,576]{1,0:T(8,128)(2,1)} %constant.51.clone.refs_2_, bf16[576,272]{1,0:T(8,128)(2,1)} %constant.52.clone.refs_3_), custom_call_target="tpu_custom_call" | custom-call | tf_op jit(solution)/shard_map/pallas_call | solution.py:151
  41.8 25.5 %shard_map.342 = (bf16[144,1024]{1,0:T(8,128)(2,1)}, bf16[576,512]{1,0:T(8,128)(2,1)}, bf16[128,16,1152]{2,1,0:T(8,128)(2,1)}, bf16[128,16,1024]{2,1,0:T(8,128)(2,1)}, bf16[128,16,1024]{2,1,0:T(8,128)(2,1)}) custom-call(s32[1]{0:T(128)} %bitcast.edge, bf16[576,512]{1,0:T(8,128)(2,1)} %shard_map.341.patches, bf16[144,1024]{1,0:T(8,128)(2,1)} %get-tuple-element.36.cotangent, ...), custom_call_target="tpu_custom_call" | custom-call | tf_op jit(solution)/shard_map/pallas_call | solution.py:374
  67.3 18.8 %shard_map.343 = (bf16[144,1024]{1,0:T(8,128)(2,1)}, bf16[576,512]{1,0:T(8,128)(2,1)}) custom-call(bf16[144,1024]{1,0:T(8,128)(2,1)} %get-tuple-element.37.refs_0_, bf16[144,144]{1,0:T(8,128)(2,1)} %constant.53.clone.refs_1_, bf16[144,144]{1,0:T(8,128)(2,1)} %constant.54.clone.refs_2_, bf16[144,144]{1,0:T(8,128)(2,1)} %constant.55.clone.refs_3_, ...), custom_call_target="tpu_custom_call" | custom-call | tf_op jit(solution)/shard_map/pallas_call | solution.py:151
  86.1 17.5 %shard_map.344 = (bf16[576,512]{1,0:T(8,128)(2,1)}, bf16[64,2,16,256]{3,2,1,0:T(8,128)(2,1)}, bf16[64,2,16,256]{3,2,1,0:T(8,128)(2,1)}, bf16[64,2,16,128]{3,2,1,0:T(8,128)(2,1)}) custom-call(s32[1]{0:T(128)} %bitcast.edge, bf16[576,512]{1,0:T(8,128)(2,1)} %get-tuple-element.34.tokens, bf16[576,512]{1,0:T(8,128)(2,1)} %get-tuple-element.40.normal, ...), custom_call_target="tpu_custom_call" | custom-call | tf_op jit(solution)/shard_map/pallas_call | solution.py:481
  103.6 13.5 %shard_map.345 = bf16[576,512]{1,0:T(8,128)(2,1)} custom-call(bf16[576,512]{1,0:T(8,128)(2,1)} %get-tuple-element.44.refs_0_, bf16[272,576]{1,0:T(8,128)(2,1)} %constant.59.clone.refs_1_, bf16[576,576]{1,0:T(8,128)(2,1)} %constant.60.clone.refs_2_, bf16[576,272]{1,0:T(8,128)(2,1)} %constant.61.clone.refs_3_), custom_call_target="tpu_custom_call" | custom-call | tf_op jit(solution)/shard_map/pallas_call | solution.py:151
  117.1 0.0 copy-start.1
  117.1 0.0 copy-start
  117.1 55.7 %shard_map.346 = (f32[16,1024]{1,0:T(8,128)}, f32[8,3072]{1,0:T(8,128)}, f32[8,1024]{1,0:T(8,128)}, f32[16,128]{1,0:T(8,128)}, f32[4,1536]{1,0:T(4,128)}, /*index=5*/f32[4,512]{1,0:T(4,128)}, f32[16,128]{1,0:T(8,128)}) custom-call(bf16[4,2,4,2,2,16,1152]{6,5,4,3,2,1,0:T(8,128)(2,1)} %bitcast.12, bf16[4,2,4,2,2,16,1024]{6,5,4,3,2,1,0:T(8,128)(2,1)} %bitcast.13, ...), custom_call_target="tpu_custom_call" | custom-call | tf_op jit(solution)/shard_map/pallas_call | solution.py:774
  172.8 1.3 slice_reduce_fusion.2
  174.1 1.4 slice_reduce_fusion.1
  175.5 1.3 slice_reduce_fusion
  176.8 0.0 copy-done.1
  176.8 0.1 reshape.71
  176.9 1.0 copy.41
  177.9 0.0 copy-done
  177.9 0.8 copy.48
  178.7 1.3 copy.49
  180.1 1.3 copy.50
  181.3 1.5 copy.51
  182.8 1.5 copy.52
  184.4 1.4 copy.53
Async XLA Ops:
  117.1 59.7 %copy-start.1 = (bf16[144,1024]{1,0:T(8,128)(2,1)S(1)}, bf16[144,1024]{1,0:T(8,128)(2,1)}, u32[]{:S(2)}) copy-start(bf16[144,1024]{1,0:T(8,128)(2,1)} %get-tuple-element.39) | copy-start | bytes 884740
  117.1 60.8 %copy-start = (bf16[576,512]{1,0:T(8,128)(2,1)S(1)}, bf16[576,512]{1,0:T(8,128)(2,1)}, u32[]{:S(2)}) copy-start(bf16[576,512]{1,0:T(8,128)(2,1)} %shard_map.345) | copy-start | bytes 1769476

commit v2 on v0

v2 whole, which is shorter than its diff:
```python
import functools
from types import SimpleNamespace

import jax
import jax.numpy as jnp
import numpy as np
from jax import lax
from jax.experimental import pallas as pl
from jax.experimental.pallas import tpu as pltpu
from jax.sharding import PartitionSpec as P

MESH = pl.DeviceIdType.MESH
HALF = jnp.bfloat16
FULL = jnp.float32
HD = 64
WH = 6
WW = 12
CELLS = 144
EPSILON = 1e-05
MASKED = -1e30
PIECES = (0, 128, 256)
PACKED = 304
LIMIT = 62 * 1024 * 1024
VMEM = pl.BlockSpec(memory_space=pltpu.VMEM)
SMEM = pl.BlockSpec(memory_space=pltpu.SMEM)
ANYWHERE = pl.BlockSpec(memory_space=pl.ANY)


def dot(left, right):
    return jnp.dot(left, right, preferred_element_type=FULL)


def dot_nt(left, right):
    return lax.dot_general(left, right, (((1,), (1,)), ((), ())), preferred_element_type=FULL)


def dot_tn(left, right):
    return lax.dot_general(left, right, (((0,), (0,)), ((), ())), preferred_element_type=FULL)


def natural_order(rows, cols):
    return lambda level, i, j: (level * rows + i) * cols + j


def window_order(rows, cols):
    def place(level, i, j):
        window = i // WH * (cols // WW) + j // WW
        return window * CELLS + ((i % WH // 3 * 2 + level) * 3 + i % 3) * WW + j % WW

    return place


def patch_order(rows, cols):
    coarse = window_order(rows // 2, cols // 2)

    def place(level, i, j):
        return (j % 2 * 2 + i % 2) * CELLS + coarse(level, i // 2, j // 2)

    return place


@functools.lru_cache(maxsize=None)
def roll_matrices(rows, cols, source, target, sign):
    orders = {"natural": natural_order, "window": window_order, "patch": patch_order}
    from_place, to_place = orders[source](rows, cols), orders[target](rows, cols)
    count = 2 * rows * cols
    pieces = ([], [], [])
    own = np.zeros((count, count), np.float32)
    for level in range(2):
        for i in range(rows):
            for j in range(cols):
                far_i, far_j = i + 3 * sign, j + 6 * sign
                across = (far_i // rows != 0, far_j // cols != 0)
                here = from_place(level, far_i % rows, far_j % cols)
                there = to_place(level, i, j)
                if across == (False, False):
                    own[there, here] = 1
                else:
                    slot = {(False, True): 0, (True, False): 1, (True, True): 2}[across]
                    pieces[slot].append((there, here))
    sizes = tuple((len(piece) + 15) // 16 * 16 for piece in pieces)
    pack = np.zeros((PACKED, count), np.float32)
    halo = np.zeros((count, PACKED), np.float32)
    for slot, piece in enumerate(pieces):
        for k, (there, here) in enumerate(piece):
            pack[PIECES[slot] + k, here] = 1
            halo[there, PIECES[slot] + k] = 1
    return pack, own, halo, sizes


def norm_parts(values):
    centre = jnp.mean(values, axis=-1, keepdims=True)
    offset = values - centre
    spread = jnp.mean(offset * offset, axis=-1, keepdims=True)
    scale = lax.rsqrt(spread + EPSILON)
    return offset * scale, scale


def norm_back(grad, normal, scale, gain):
    inner = grad * gain
    mean = jnp.mean(inner, axis=-1, keepdims=True)
    along = jnp.mean(inner * normal, axis=-1, keepdims=True)
    return (inner - mean - normal * along) * scale


def two_heads(pair):
    first = lax.broadcasted_iota(jnp.int32, pair.shape, 1) < HD
    zero = jnp.zeros_like(pair)
    return jnp.concatenate([jnp.where(first, pair, zero), jnp.where(first, zero, pair)], axis=0)


def one_pair(stack):
    half = stack.shape[0] // 2
    first = lax.broadcasted_iota(jnp.int32, (half, 2 * HD), 1) < HD
    return jnp.where(first, stack[:half], stack[half:])


def pair_mask(edge):
    shape = (CELLS, 2 * CELLS)
    key = lax.broadcasted_iota(jnp.int32, shape, 0)
    query = lax.broadcasted_iota(jnp.int32, shape, 1)
    query = jnp.where(query >= CELLS, query - CELLS, query)
    apart = (key < CELLS // 2) != (query < CELLS // 2)
    return jnp.where(apart, edge, 0) > 0


def pair_weights(queries, keys, mask):
    scores = dot_nt(keys, queries * 0.125)
    scores = jnp.where(mask, MASKED, scores)
    powers = jnp.exp(scores - jnp.max(scores, axis=0, keepdims=True))
    return powers * (1.0 / jnp.sum(powers, axis=0, keepdims=True))


def pair_forward(weights, values):
    return one_pair(dot_tn(weights.astype(HALF), values)).astype(HALF)


def pair_back(weights, queries, keys, values, upstream):
    weight_grad = dot_nt(values, upstream)
    inner = jnp.sum(weights * weight_grad, axis=0, keepdims=True)
    score_grad = (weights * (weight_grad - inner) * 0.125).astype(HALF)
    query_grad = one_pair(dot_tn(score_grad, keys)).astype(HALF)
    key_grad = dot(score_grad, queries).astype(HALF)
    value_grad = dot(weights.astype(HALF), upstream).astype(HALF)
    return query_grad, key_grad, value_grad


def four_stacked(pieces):
    rows, width = pieces[0].shape
    shaped = [piece.reshape(rows // 8, 8, width) for piece in pieces]
    upper = lax.broadcasted_iota(jnp.int32, shaped[0].shape, 1) < 4
    turned = [pltpu.roll(piece, 4, 1) for piece in shaped]
    even = [jnp.where(upper, shaped[n], turned[n + 1]) for n in (0, 2)]
    odd = [jnp.where(upper, turned[n], shaped[n + 1]) for n in (0, 2)]
    return [jnp.concatenate(pair, axis=1).astype(HALF) for pair in (even, odd)]


ORDERS = (("x", "y", "z"), ("y", "z", "x"), ("z", "x", "y"))
LEADS = (((4, 2, 2), (2, 2)), ((2, 4, 2), (4,)), ((4, 4), (4,)))
WIDTHS = (1152, 1024, 1024, 256, 256, 128)
LON, LAT, DIAG = 0, 1, 2
STEPS = ((0, 1), (1, 0), (1, 1))


def device_at(place, core):
    lat = place["y"] * 2 + place["z"] // 2
    lon = place["x"] * 4 + place["z"] % 2 * 2 + core
    return (lat, lon)


def along(place, axis, steps):
    moved = dict(place)
    moved[axis] = lax.rem(place[axis] + steps, 4)
    return moved


def first_cut(kind, ref, index):
    if kind == 0:
        return ref.at[:, :, index]
    if kind == 1:
        return ref.at[index]
    return ref.at[:, index // 2, :, index % 2]


def second_cut(kind, ref, index):
    if kind == 0:
        return ref.at[index]
    if kind == 1:
        return ref.at[index // 2, :, index % 2]
    return ref.at[:, index]


def third_cut(kind, ref, index):
    if kind == 0:
        return ref.at[index // 2, index % 2]
    return ref.at[index]


def spots(lead, i):
    found = []
    for size in reversed(lead):
        found.insert(0, i % size)
        i = i // size
    return tuple(found)


def added(base, arrivals):
    total = base.astype(FULL)
    for arrival in arrivals:
        total = total + arrival.astype(FULL)
    return total


def of(r, name, p):
    return getattr(r, name + str(p))


def owner_pick(rows_each, core):
    shift = rows_each.bit_length() - 1
    feature = lax.broadcasted_iota(jnp.int32, (256, 128), 0)
    place = lax.broadcasted_iota(jnp.int32, (256, 128), 1)
    wanted = ((place >> shift) << (shift + 1)) + (place & (rows_each - 1)) + core * rows_each
    return jnp.where(feature == wanted, 1.0, 0.0).astype(HALF)


def in_two(row):
    high = row.astype(HALF)
    low = (row - high.astype(FULL)).astype(HALF)
    place = lax.broadcasted_iota(jnp.int32, (16, row.shape[1]), 0)
    wide_high = jnp.broadcast_to(high.astype(FULL), place.shape)
    wide_low = jnp.broadcast_to(low.astype(FULL), place.shape)
    return jnp.where(place == 0, wide_high, jnp.where(place == 1, wide_low, 0.0)).astype(HALF)


def whole_kernel(names, summing, *refs):
    r = SimpleNamespace(**dict(zip(names, refs)))
    lat, lon = lax.axis_index("lat"), lax.axis_index("lon")
    lats, lons = lax.axis_size("lat"), lax.axis_size("lon")
    core = lon % 2
    place = {"y": lat // 2, "x": lon // 4, "z": lat % 2 * 2 + lon // 2 % 2}
    sibling = (lat, lon + 1 - 2 * core)
    edge = jnp.where(lat == lats - 1, 1, 0)
    used = [0]

    def remote(source, target, device):
        slot = used[0]
        used[0] += 1
        copy = pltpu.make_async_remote_copy(
            src_ref=source,
            dst_ref=target,
            send_sem=r.send_sem.at[slot],
            recv_sem=r.recv_sem.at[slot],
            device_id=device,
            device_id_type=MESH,
        )
        copy.start()
        return copy

    def neighbour(step, way):
        return (
            lax.rem(lat + lats + way * step[0], lats),
            lax.rem(lon + lons + way * step[1], lons),
        )

    loads = {}

    def load(name):
        slot = LOADED.index(name)
        loads[name] = pltpu.make_async_copy(getattr(r, name + "_any"), getattr(r, name), r.load_sem.at[slot])
        loads[name].start()

    for kind, held in (("back", "in"), ("end", "mid")):
        for matrix in ("_pack", "_own", "_halo"):
            setattr(r, kind + matrix, getattr(r, held + matrix))
    r.patches_grad = r.fine_out
    for name in LOADED[:11]:
        load(name)

    barrier = pltpu.get_barrier_semaphore()
    partners = [neighbour(step, way) for step in STEPS for way in (1, -1)] + [sibling]
    if summing:
        partners += [
            device_at(along(place, axis, k), core) for axis in ("x", "y", "z") for k in (1, 2, 3)
        ]
    for partner in partners:
        pl.semaphore_signal(barrier, inc=1, device_id=partner, device_id_type=MESH)

    def pack_piece(kind, value, slot, size):
        rows = slice(PIECES[slot], PIECES[slot] + size)
        getattr(r, kind + "_packed")[rows, :] = dot(getattr(r, kind + "_pack")[rows, :], value).astype(HALF)

    def send_piece(kind, slot, size, sign):
        rows = pl.ds(PIECES[slot], size)
        return remote(
            getattr(r, kind + "_packed").at[rows],
            getattr(r, kind + "_landed").at[rows],
            neighbour(STEPS[slot], -sign),
        )

    def gathered(kind, rows, value, sizes, needed):
        total = dot(getattr(r, kind + "_own")[rows, :], value)
        for slot in needed:
            piece = slice(PIECES[slot], PIECES[slot] + sizes[slot])
            total = total + dot(getattr(r, kind + "_halo")[rows, piece], getattr(r, kind + "_landed")[piece, :])
        return total

    fine_sizes, coarse_sizes = (112, 112, 48), (48, 48, 48)
    loads["in_pack"].wait()
    for slot in (LAT, DIAG, LON):
        pack_piece("in", r.tokens[...], slot, fine_sizes[slot])
    for slot in (LAT, DIAG, LON):
        pack_piece("cot", r.cotangent[...], slot, coarse_sizes[slot])
    pl.semaphore_wait(barrier, len(partners))
    arrive = {slot: send_piece("in", slot, fine_sizes[slot], 1) for slot in (LAT, DIAG, LON)}
    cot_arrive = [send_piece("cot", slot, coarse_sizes[slot], 1) for slot in (LAT, DIAG, LON)]
    r.fine_out[...] = jnp.zeros_like(r.fine_out)
    r.tokens_back[...] = jnp.zeros_like(r.tokens_back)

    keep4, give4 = owner_pick(4, core), owner_pick(4, 1 - core)
    keep8, give8 = owner_pick(8, core), owner_pick(8, 1 - core)
    keep16, give16 = owner_pick(16, core), owner_pick(16, 1 - core)

    def split(value, keep, give, name, rows):
        for block in range(value.shape[1] // 256):
            part = value[:, 256 * block : 256 * block + 256]
            cols = slice(128 * block, 128 * block + 128)
            getattr(r, name + "_left")[rows, cols] = dot(part, keep).astype(HALF)
            getattr(r, name + "_give")[rows, cols] = dot(part, give).astype(HALF)

    def hand_left(name):
        count = getattr(r, name + "_give").shape[0]
        return remote(getattr(r, name + "_give"), getattr(r, name + "_left").at[pl.ds(count, count)], sibling)

    def hand_right(name, start, size):
        half = getattr(r, name).shape[0] // 2
        held = getattr(r, name)
        return remote(held.at[pl.ds(start, size)], held.at[pl.ds(half + start, size)], sibling)

    handed_fine, handed_coarse, late = [], [], []

    needs = ((), (LON,), (LAT,), (LON, LAT, DIAG))
    waited = set()
    mid_arrive = []
    for name in ("in_own", "in_halo", "qkv_f", "proj_f", "mid_pack"):
        loads[name].wait()
    for w in range(4):
        for slot in needs[w]:
            if slot not in waited:
                arrive[slot].wait()
                waited.add(slot)
        rows = slice(CELLS * w, CELLS * w + CELLS)
        values = gathered("in", rows, r.tokens[...], fine_sizes, needs[w])
        r.rolled[rows, :] = values.astype(HALF)
        unit, _ = norm_parts(values)
        normed = (unit * r.gain_f[...]).astype(HALF)
        split(normed, keep4, give4, "normal", rows)
        qkv = r.qkv
        for n in range(3):
            cols = slice(512 * n, 512 * n + 512)
            qkv[rows, cols] = dot(normed, r.qkv_f[:, cols]).astype(HALF)
        mask = pair_mask(edge if w >= 2 else 0)
        for p in range(4):
            at = 128 * p
            queries = two_heads(qkv[rows, at : at + 128])
            weights = pair_weights(queries, qkv[rows, 512 + at : 640 + at], mask)
            r.attended[rows, at : at + 128] = pair_forward(
                weights, qkv[rows, 1024 + at : 1152 + at]
            )
        attended = r.attended[rows, :]
        split(attended, keep4, give4, "attended", rows)
        r.fine_out[rows, :] = (values + dot(attended, r.proj_f[...])).astype(HALF)
        for slot in {1: (LAT,), 2: (DIAG, LON)}.get(w, ()):
            pack_piece("mid", r.fine_out[...], slot, fine_sizes[slot])
            mid_arrive.append(send_piece("mid", slot, fine_sizes[slot], 1))
    handed_fine += [hand_left("normal"), hand_left("attended")]
    for name in LOADED[11:14]:
        load(name)

    for copy in cot_arrive:
        copy.wait()
    every = slice(None)
    cot = gathered("cot", every, r.cotangent[...], coarse_sizes, (LON, LAT, DIAG)).astype(HALF)
    own = slice(0, CELLS)
    r.cot_right[own, :] = cot
    handed_coarse.append(hand_right("cot_right", 0, CELLS))
    loads["proj_c"].wait()
    r.cot_attended[...] = dot_nt(cot, r.proj_c[...]).astype(HALF)
    loads["mid_own"].wait()
    loads["mid_halo"].wait()
    for copy in mid_arrive:
        copy.wait()
    values = jnp.concatenate(
        [
            gathered(
                "mid",
                slice(CELLS * g, CELLS * g + CELLS),
                r.fine_out[...],
                fine_sizes,
                (LON, LAT, DIAG),
            )
            for g in range(4)
        ],
        axis=1,
    )
    for name in LOADED[14:]:
        load(name)
    unit, scale_merge = norm_parts(values)
    r.unit_merge[...] = unit
    merged = (unit * r.gain_m[...]).astype(HALF)
    loads["merge_w"].wait()
    coarse_in = dot(merged, r.merge_w[...]).astype(HALF).astype(FULL)
    split(merged, keep16, give16, "merged", own)
    merged_handed = hand_left("merged")
    unit, scale_coarse = norm_parts(coarse_in)
    r.unit_coarse[...] = unit
    normed = (unit * r.gain_c[...]).astype(HALF)
    loads["qkv_c"].wait()
    for n in range(3):
        cols = slice(1024 * n, 1024 * (n + 1))
        r.qkv_coarse[:, cols] = dot(normed, r.qkv_c[:, cols]).astype(HALF)
    split(normed, keep8, give8, "normed", own)
    handed_coarse.append(hand_left("normed"))
    qkv = r.qkv_coarse
    mask = pair_mask(edge)
    for p in range(8):
        at = 128 * p
        queries = two_heads(qkv[:, at : at + 128])
        keys, worth = qkv[:, 1024 + at : 1152 + at], qkv[:, 2048 + at : 2176 + at]
        weights = pair_weights(queries, keys, mask)
        r.coarse_attended[:, at : at + 128] = pair_forward(weights, worth)
        upstream = two_heads(r.cot_attended[:, at : at + 128])
        grads = pair_back(weights, queries, keys, worth, upstream)
        for n in range(3):
            r.qkv_right[own, 1024 * n + at : 1024 * n + at + 128] = grads[n]
    handed_coarse.append(hand_right("qkv_right", 0, CELLS))
    attended = r.coarse_attended[...]
    split(attended, keep8, give8, "coarse", own)
    handed_coarse.append(hand_left("coarse"))
    normed_grad = dot_nt(r.qkv_right[own, :], r.qkv_c[...]).astype(HALF).astype(FULL)
    gain_row = jnp.sum(normed_grad * r.unit_coarse[...], axis=0, keepdims=True)
    split(in_two(gain_row), keep8, give8, "gain_coarse", slice(0, 16))
    gains_handed = [hand_left("gain_coarse")]
    coarse_grad = r.cot_right[own, :].astype(FULL) + norm_back(
        normed_grad, r.unit_coarse[...], scale_coarse, r.gain_c[...]
    )
    r.inner_right[own, :] = coarse_grad.astype(HALF)
    inner_handed = hand_right("inner_right", 0, CELLS)
    merged_grad = dot_nt(r.inner_right[own, :], r.merge_w[...]).astype(HALF).astype(FULL)
    gain_row = jnp.sum(merged_grad * r.unit_merge[...], axis=0, keepdims=True)
    split(in_two(gain_row), keep16, give16, "gain_merge", slice(0, 16))
    gains_handed.append(hand_left("gain_merge"))
    back = norm_back(merged_grad, r.unit_merge[...], scale_merge, r.gain_m[...]).astype(HALF)
    for g in range(4):
        r.patches_grad[CELLS * g : CELLS * (g + 1), :] = back[:, 512 * g : 512 * (g + 1)]
    for name in ("back_pack", "back_own", "back_halo"):
        loads[name].wait()
    back_arrive = {}
    for slot in (LAT, DIAG, LON):
        pack_piece("back", r.patches_grad[...], slot, fine_sizes[slot])
        back_arrive[slot] = send_piece("back", slot, fine_sizes[slot], -1)
    r.coarse_out[...] = (coarse_in + dot(attended, r.proj_c[...])).astype(HALF)
    for slot in (LAT, DIAG, LON):
        pack_piece("out", r.coarse_out[...], slot, coarse_sizes[slot])
    out_arrive = [send_piece("out", slot, coarse_sizes[slot], -1) for slot in (LAT, DIAG, LON)]

    sums = {}

    def start_first(p):
        axis = ORDERS[p % 3][0]
        sums[p] = []
        for k in (2, 1, 3):
            moved = along(place, axis, k)
            sums[p].append(
                remote(
                    first_cut(p % 3, of(r, "share", p), moved[axis]),
                    of(r, "landed0_", p).at[k - 1],
                    device_at(moved, core),
                )
            )

    def start_second(p):
        for copy in sums[p]:
            copy.wait()
        mine = first_cut(p % 3, of(r, "share", p), place[ORDERS[p % 3][0]])

        def add(i, carry):
            at = spots(LEADS[p % 3][0], i)
            total = added(mine[at], [of(r, "landed0_", p)[(k,) + at] for k in range(3)])
            of(r, "landed0_", p)[(0,) + at] = total.astype(HALF)
            return carry

        lax.fori_loop(0, 16, add, 0)
        axis = ORDERS[p % 3][1]
        sums[p] = []
        for k in (2, 1, 3):
            moved = along(place, axis, k)
            sums[p].append(
                remote(
                    second_cut(p % 3, of(r, "landed0_", p).at[0], moved[axis]),
                    of(r, "landed1_", p).at[k - 1],
                    device_at(moved, core),
                )
            )

    def start_third(p):
        for copy in sums[p]:
            copy.wait()
        mine = second_cut(p % 3, of(r, "landed0_", p).at[0], place[ORDERS[p % 3][1]])
        total = added(mine[...], [of(r, "landed1_", p)[k] for k in range(3)])
        of(r, "summed1_", p)[...] = total.astype(HALF)
        axis = ORDERS[p % 3][2]
        sums[p] = []
        for k in (2, 1, 3):
            moved = along(place, axis, k)
            sums[p].append(
                remote(
                    third_cut(p % 3, of(r, "summed1_", p), moved[axis]),
                    of(r, "landed2_", p).at[k - 1],
                    device_at(moved, core),
                )
            )

    def finish(p):
        for copy in sums[p]:
            copy.wait()
        mine = third_cut(p % 3, of(r, "summed1_", p), place[ORDERS[p % 3][2]])
        total = added(mine[...], [of(r, "landed2_", p)[k] for k in range(3)])
        of(r, "sum", p)[...] = total

    for copy in handed_coarse:
        copy.wait()

    def paired(grad, lead):
        width = grad.shape[1] // 2
        rows = grad.shape[0] // 8
        pieces = [grad[:, :width].reshape(rows, 8, width), grad[:, width:].reshape(rows, 8, width)]
        return jnp.concatenate(pieces, axis=1).astype(HALF).reshape(lead + (16, width))

    def qkv_rows(n, carry):
        cols = pl.ds(pl.multiple_of(n * 256, 256), 256)
        left = r.normed_left[:, cols]
        for low, share, at in ((0, 1, 0), (512, 1, 512), (1024, 2, 0)):
            right = jnp.concatenate(
                [
                    r.qkv_right[:, low : low + 512],
                    r.qkv_right[:, low + 1536 : low + 2048],
                ],
                axis=1,
            )
            of(r, "share", share)[pl.ds(n * 2, 2), :, :, :, :, at : at + 512] = paired(
                dot_tn(left, right), (2, 2, 4, 2)
            )
        grad = dot_tn(r.coarse_left[:, cols], r.cot_right[...])
        r.share2[pl.ds(n * 2, 2), :, :, :, :, 512:] = paired(grad, (2, 2, 4, 2))
        return carry

    lax.fori_loop(0, 2, qkv_rows, 0)
    if summing:
        start_first(1)
        start_first(2)
    for copy in gains_handed + [merged_handed, inner_handed]:
        copy.wait()
    ones = jnp.ones((32, 128), HALF)
    left_lane = lax.broadcasted_iota(jnp.int32, (64, 16, 128), 2) < HD
    by_merge = dot_tn(r.gain_merge_left[...], ones).reshape(64, 16, 128)
    by_coarse = dot_tn(r.gain_coarse_left[...], ones).reshape(64, 8, 128)
    by_coarse = jnp.concatenate([by_coarse, by_coarse], axis=1)
    gains = jnp.where(left_lane, by_merge, by_coarse).astype(HALF)
    r.share0[:, :, :, :, :, 1024:] = gains.reshape(4, 2, 4, 2, 16, 128)

    def merge_rows(n, carry):
        left = r.merged_left[:, pl.ds(pl.multiple_of(n * 256, 256), 256)]
        grad = dot_tn(left, r.inner_right[...])
        r.share0[n, :, :, :, :, :1024] = grad.astype(HALF).reshape(2, 4, 2, 16, 1024)
        return carry

    lax.fori_loop(0, 4, merge_rows, 0)
    if summing:
        start_first(0)

    needs = ((LON, LAT, DIAG), (LAT,), (LON,), ())
    waited = set()
    end_arrive = []
    gain_row = jnp.zeros((1, 512), FULL)
    for w in (3, 2, 1, 0):
        for slot in needs[w]:
            if slot not in waited:
                back_arrive[slot].wait()
                waited.add(slot)
        rows = slice(CELLS * w, CELLS * w + CELLS)
        grad = gathered("back", rows, r.patches_grad[...], fine_sizes, needs[w]).astype(HALF)
        r.fine_right[rows, :] = grad
        handed_fine.append(hand_right("fine_right", CELLS * w, CELLS))
        attended_grad = dot_nt(grad, r.proj_f[...]).astype(HALF)
        qkv = r.qkv
        mask = pair_mask(edge if w >= 2 else 0)
        for p in range(4):
            at = 128 * p
            queries = two_heads(qkv[rows, at : at + 128])
            keys, worth = qkv[rows, 512 + at : 640 + at], qkv[rows, 1024 + at : 1152 + at]
            weights = pair_weights(queries, keys, mask)
            upstream = two_heads(attended_grad[:, at : at + 128])
            grads = pair_back(weights, queries, keys, worth, upstream)
            for n in range(3):
                r.triple_right[rows, 512 * n + at : 512 * n + at + 128] = grads[n]
        handed_fine.append(hand_right("triple_right", CELLS * w, CELLS))
        normed_grad = dot_nt(r.triple_right[rows, :], r.qkv_f[...]).astype(HALF).astype(FULL)
        unit, scale = norm_parts(r.rolled[rows, :].astype(FULL))
        gain_row = gain_row + jnp.sum(normed_grad * unit, axis=0, keepdims=True)
        back = norm_back(normed_grad, unit, scale, r.gain_f[...])
        r.tokens_back[rows, :] = (grad.astype(FULL) + back).astype(HALF)
        for slot in {2: (LAT,), 1: (DIAG, LON)}.get(w, ()):
            if not end_arrive:
                loads["end_pack"].wait()
            pack_piece("end", r.tokens_back[...], slot, fine_sizes[slot])
            end_arrive.append(send_piece("end", slot, fine_sizes[slot], -1))
    split(in_two(gain_row), keep4, give4, "gain_fine", slice(0, 16))
    handed_fine.append(hand_left("gain_fine"))
    for copy in handed_fine:
        copy.wait()

    def fine_rows(n, carry):
        cols = pl.ds(pl.multiple_of(n * 128, 128), 128)

        def store(p, at, pieces):
            width = pieces[0].shape[1]
            for side, value in enumerate(four_stacked(pieces)):
                of(r, "share", p)[pl.ds(n * 2, 2), :, :, side, :, at : at + width] = value.reshape(
                    2, 2, 4, 16, width
                )

        grad = dot_tn(r.normal_left[:, cols], r.triple_right[...])
        store(3, 0, [grad[:, 384 * m : 384 * m + 256] for m in range(4)])
        store(4, 0, [grad[:, 384 * m + 256 : 384 * m + 384] for m in range(4)])
        grad = dot_tn(r.attended_left[:, cols], r.fine_right[...])
        store(4, 128, [grad[:, 128 * m : 128 * m + 128] for m in range(4)])
        store(5, 0, [dot_tn(r.gain_fine_left[:, cols], ones)] * 4)
        return carry

    lax.fori_loop(0, 2, fine_rows, 0)
    if summing:
        for p in (3, 4, 5):
            start_first(p)
        for p in (1, 2, 0):
            start_second(p)
    for copy in out_arrive:
        copy.wait()
    for name in ("end_own", "end_halo"):
        loads[name].wait()
    r.coarse_tokens[...] = gathered(
        "out", every, r.coarse_out[...], coarse_sizes, (LON, LAT, DIAG)
    ).astype(HALF)
    if summing:
        for p in (3, 4, 5):
            start_second(p)
    for copy in end_arrive:
        copy.wait()
    r.tokens_grad[...] = gathered(
        "end", every, r.tokens_back[...], fine_sizes, (LON, LAT, DIAG)
    ).astype(HALF)
    if summing:
        for p in (1, 2, 0, 3, 4, 5):
            start_third(p)
        for p in (1, 2, 0, 3, 4, 5):
            finish(p)
    else:
        for p in range(6):
            of(r, "sum", p)[...] = of(r, "share", p)[...].reshape(64, 16, WIDTHS[p])


LOADED = tuple(
    dict(
        in_pack=0,
        in_own=0,
        in_halo=0,
        qkv_f=0,
        proj_f=0,
        mid_pack=0,
        proj_c=0,
        mid_own=0,
        mid_halo=0,
        merge_w=0,
        qkv_c=0,
        back_pack=0,
        back_own=0,
        back_halo=0,
        end_pack=0,
        end_own=0,
        end_halo=0,
    )
)


def whole(values, summing):
    inputs, scratch, outputs = [], [], []

    def matrices(kind, rows, cols, source, target, sign):
        pack, own, halo, _ = roll_matrices(rows, cols, source, target, sign)
        return {
            kind + "_pack": jnp.asarray(pack, HALF),
            kind + "_own": jnp.asarray(own, HALF),
            kind + "_halo": jnp.asarray(halo, HALF),
        }

    values = dict(values)
    values.update(matrices("in", 12, 24, "natural", "window", 1))
    values.update(matrices("cot", 6, 12, "natural", "window", 1))
    values.update(matrices("mid", 12, 24, "window", "patch", 1))
    values.update(matrices("back", 12, 24, "patch", "window", -1))
    values.update(matrices("end", 12, 24, "window", "natural", -1))
    values.update(matrices("out", 6, 12, "window", "natural", -1))
    specs, operands = [], []
    for name, value in values.items():
        loaded = name in LOADED
        inputs.append(name + "_any" if loaded else name)
        specs.append(ANYWHERE if loaded else VMEM)
        operands.append(value)
    half = {name: values[name].shape for name in LOADED[:11]}
    for kind, width in (("in", 512), ("cot", 1024), ("mid", 512), ("back", 512), ("end", 512), ("out", 1024)):
        half[kind + "_packed"] = half[kind + "_landed"] = (PACKED, width)
    lefts = dict(
        normal=(576, 256),
        attended=(576, 256),
        merged=(CELLS, 1024),
        normed=(CELLS, 512),
        coarse=(CELLS, 512),
        gain_coarse=(16, 512),
        gain_merge=(16, 1024),
        gain_fine=(16, 256),
    )
    for name, (count, width) in lefts.items():
        half[name + "_left"] = (2 * count, width)
        half[name + "_give"] = (count, width)
    half.update(
        rolled=(576, 512),
        qkv=(576, 1536),
        attended=(576, 512),
        fine_out=(576, 512),
        tokens_back=(576, 512),
        cot_right=(2 * CELLS, 1024),
        cot_attended=(CELLS, 1024),
        qkv_coarse=(CELLS, 3072),
        coarse_attended=(CELLS, 1024),
        coarse_out=(CELLS, 1024),
        qkv_right=(2 * CELLS, 3072),
        inner_right=(2 * CELLS, 1024),
        fine_right=(1152, 512),
        triple_right=(1152, 1536),
    )
    for p, width in enumerate(WIDTHS):
        half["share" + str(p)] = (4, 2, 4, 2, 16, width)
        if summing:
            first, second = LEADS[p % 3]
            half["landed0_" + str(p)] = (3,) + first + (16, width)
            half["landed1_" + str(p)] = (3,) + second + (16, width)
            half["landed2_" + str(p)] = (3, 16, width)
            half["summed1_" + str(p)] = second + (16, width)
    memory = {name: pltpu.VMEM(shape, HALF) for name, shape in half.items()}
    memory["unit_merge"] = pltpu.VMEM((CELLS, 2048), FULL)
    memory["unit_coarse"] = pltpu.VMEM((CELLS, 1024), FULL)
    memory["send_sem"] = pltpu.SemaphoreType.DMA((100,))
    memory["recv_sem"] = pltpu.SemaphoreType.DMA((100,))
    memory["load_sem"] = pltpu.SemaphoreType.DMA((len(LOADED),))
    outputs = {
        "coarse_tokens": jax.ShapeDtypeStruct((CELLS, 1024), HALF),
        "tokens_grad": jax.ShapeDtypeStruct((576, 512), HALF),
    }
    for p, width in enumerate(WIDTHS):
        outputs["sum" + str(p)] = (
            jax.ShapeDtypeStruct((16, width), FULL)
            if summing
            else jax.ShapeDtypeStruct((64, 16, width), HALF)
        )
    names = tuple(inputs) + tuple(outputs) + tuple(memory)
    results = pl.pallas_call(
        functools.partial(whole_kernel, names, summing),
        out_shape=list(outputs.values()),
        in_specs=specs,
        out_specs=[VMEM] * len(outputs),
        scratch_shapes=list(memory.values()),
        compiler_params=pltpu.CompilerParams(
            collective_id=1, has_side_effects=True, vmem_limit_bytes=LIMIT
        ),
    )(*operands)
    return dict(zip(outputs, results))


def prepared(
    tokens,
    cotangent,
    gain_fine,
    qkv_fine,
    proj_fine,
    gain_merge,
    merge_weight,
    gain_coarse,
    qkv_coarse,
    proj_coarse,
):
    return dict(
        tokens=tokens.reshape(576, 512),
        cotangent=cotangent.reshape(CELLS, 1024),
        gain_f=gain_fine.reshape(1, 512),
        gain_m=gain_merge.reshape(1, 2048),
        gain_c=gain_coarse.reshape(1, 1024),
        qkv_f=qkv_fine,
        proj_f=proj_fine,
        merge_w=merge_weight,
        qkv_c=qkv_coarse,
        proj_c=proj_coarse,
    )


def last_kernel(*refs):
    coarse, tokens, a, b, c, d, e, f = refs[:8]
    coarse_out, tokens_out, fine_gain, qkv_f, proj_f, merge_gain, merge, coarse_gain, qkv_c, proj_c = refs[8:]
    coarse_out[...] = coarse[...]
    tokens_out[...] = tokens[...]

    def across(column, count):
        row = lax.broadcasted_iota(jnp.int32, (16, 128), 0)
        lane = lax.broadcasted_iota(jnp.int32, (16, 128), 1)
        line = jnp.sum(jnp.where(row == lane, column, 0.0), axis=0, keepdims=True)
        return line[:, :count]

    block = a[:, 1024:]
    merge_gain[...] = across(jnp.broadcast_to(block[:, :1], (16, 128)), 16)
    coarse_gain[...] = across(jnp.broadcast_to(block[:, HD : HD + 1], (16, 128)), 8)
    fine_gain[...] = across(f[...], 4)
    merge[...] = a[:, :1024]
    for n in range(2):
        rows = slice(8 * n, 8 * n + 8)
        qkv_c[:, 1536 * n : 1536 * n + 1024] = b[rows, :]
        qkv_c[:, 1536 * n + 1024 : 1536 * n + 1536] = c[rows, :512]
        proj_c[:, 512 * n : 512 * n + 512] = c[rows, 512:]
    for n in range(4):
        rows = slice(4 * n, 4 * n + 4)
        qkv_f[:, 384 * n : 384 * n + 256] = d[rows, :]
        qkv_f[:, 384 * n + 256 : 384 * n + 384] = e[rows, :128]
        proj_f[:, 128 * n : 128 * n + 128] = e[rows, 128:]


def last(found):
    shapes = [jax.ShapeDtypeStruct((CELLS, 1024), HALF), jax.ShapeDtypeStruct((576, 512), HALF)]
    shapes += [
        jax.ShapeDtypeStruct(shape, FULL)
        for shape in (
            (1, 4),
            (4, 1536),
            (4, 512),
            (1, 16),
            (16, 1024),
            (1, 8),
            (8, 3072),
            (8, 1024),
        )
    ]
    outs = pl.pallas_call(
        last_kernel, out_shape=shapes, in_specs=[VMEM] * 8, out_specs=[VMEM] * 10
    )(*found)
    outs = list(outs)
    outs[0] = outs[0].reshape(2, 6, 12, 1024)
    outs[1] = outs[1].reshape(2, 12, 24, 512)
    for n in (2, 5, 7):
        outs[n] = outs[n].reshape(-1)
    return tuple(outs)


def local(*args):
    found = whole(prepared(*args), True)
    return last(tuple(found.values()))


def solution(mesh):
    grid = P(None, "lat", "lon", None)
    vector, matrix = P(("lat", "lon")), P(("lat", "lon"), None)
    return jax.shard_map(
        local,
        mesh=mesh,
        in_specs=(grid, grid) + (P(),) * 8,
        out_specs=(grid, grid, vector, matrix, matrix, vector, matrix, vector, matrix, matrix),
        check_vma=False,
    )
```

time: 2410 us -> 103 us (0.04)
  waiting for transfers between devices: 2030 us -> 0 us
  local copies, waits for them, and re-layouts: 127 us -> 3.86 us
  matrix products: 104 us -> 0 us
  Pallas kernels: 0 us -> 98.4 us
  blocking collectives: 62.9 us -> 0 us
  other arithmetic: 35.1 us -> 0 us
  starting transfers between devices: 28.2 us -> 0 us
    reduce_scatter x3 -> x0, waiting for transfers between devices: 1940 us -> none  [the longest x1 654 us: local(): lax.psum_scatter(qkv_coarse_grad, ('lat', 'lon'), scatter_dimension=0, ti...]
    dot_general x26 -> x0, matrix products: 99.5 us -> none  [the longest x5 24.5 us: weight_gradient(): jnp.dot(as_rows(left_grid).T, as_rows(right_grid), preferred_element_type...]
    pallas_call x0 -> x2, Pallas kernels: none -> 98.4 us  [the longest x1 96.2 us: whole(): pl.pallas_call(functools.partial(whole_kernel, names, summing), out_shape...]
    ppermute x16 -> x0, waiting for transfers between devices: 67 us -> none  [shifted(): return lax.ppermute(value, axis, pairs)]
    unnamed x1 -> x0, blocking collectives: 62.9 us -> none
    another operation x13 -> x0, local copies, waits for them, and re-layouts: 49.7 us -> none  [the longest x2 10.8 us: attend_back(): jnp.stack([query_grad, key_grad, value_grad], axis=2)]
    ppermute x16 -> x0, starting transfers between devices: 27.8 us -> none  [shifted(): return lax.ppermute(value, axis, pairs)]
  transfers between devices with their start and end apart: 20 -> 0, of which waited for: 17 -> 0; matrix products, arithmetic and copies ran while one was open for 3% -> 0% of each run, Pallas kernels for 0% -> 0%
where the time goes in v2:
time: 103 us
  Pallas kernels  98.4 us (96%)
  local copies, waits for them, and re-layouts  3.86 us (4%)
    pallas_call x1, Pallas kernels, whole(): pl.pallas_call(functools.partial(whole_kernel, names, summing), out_shape...  96.2 us
    pallas_call x1, Pallas kernels, last(): pl.pallas_call(last_kernel, out_shape=shapes, in_specs=[VMEM] * 8, out_sp...  2.27 us

profile of v2, /device:TPU:0, one launch (start us, length us, event | category | flops | bytes accessed | tf_op | source)
XLA Modules:
  0.0 103.0 jit_solution(2459364896141040496)
XLA Ops:
  0.6 1.0 %copy.40 = bf16[2,6,12,1024]{3,2,1,0:T(8,128)(2,1)S(1)} copy(bf16[2,6,12,1024]{3,0,2,1:T(2,128)(2,1)} %param.29) | data formatting | bytes 589824 | tf_op args[1]
  1.7 0.8 reshape.51.refs_1_
  2.5 96.2 %shard_map.339 = (bf16[144,1024]{1,0:T(8,128)(2,1)}, bf16[576,512]{1,0:T(8,128)(2,1)}, f32[16,1152]{1,0:T(8,128)}, f32[16,1024]{1,0:T(8,128)}, f32[16,1024]{1,0:...) custom-call(bf16[576,512]{1,0:T(8,128)(2,1)} %bitcast.8, bf16[144,1024]{1,0:T(8,128)(2,1)} %reshape.51.refs_1_, ...), custom_call_target="tpu_custom_call" | custom-call | tf_op jit(solution)/shard_map/pallas_call | solution.py:775
  98.6 2.3 %shard_map.340 = (bf16[144,1024]{1,0:T(8,128)(2,1)}, bf16[576,512]{1,0:T(8,128)(2,1)}, f32[1,4]{1,0:T(1,128)}, f32[4,1536]{1,0:T(4,128)}, f32[4,512]{1,0:T(4,128...) custom-call(bf16[144,1024]{1,0:T(8,128)(2,1)} %get-tuple-element.28.ref, ...), custom_call_target="tpu_custom_call" | custom-call | tf_op jit(solution)/shard_map/pallas_call | solution.py:858
  100.9 1.0 reshape.55
  101.9 1.0 copy.41

commit v3 on v2

--- a/solution.py
+++ b/solution.py
@@ -42,6 +42,10 @@
     return lambda level, i, j: (level * rows + i) * cols + j
 
 
+def level_last_order(rows, cols):
+    return lambda level, i, j: (i * cols + j) * 2 + level
+
+
 def window_order(rows, cols):
     def place(level, i, j):
         window = i // WH * (cols // WW) + j // WW
@@ -61,7 +65,7 @@
 
 @functools.lru_cache(maxsize=None)
 def roll_matrices(rows, cols, source, target, sign):
-    orders = {"natural": natural_order, "window": window_order, "patch": patch_order}
+    orders = {"last": level_last_order, "natural": natural_order, "window": window_order, "patch": patch_order}
     from_place, to_place = orders[source](rows, cols), orders[target](rows, cols)
     count = 2 * rows * cols
     pieces = ([], [], [])
@@ -131,17 +135,17 @@
     return powers * (1.0 / jnp.sum(powers, axis=0, keepdims=True))
 
 
-def pair_forward(weights, values):
-    return one_pair(dot_tn(weights.astype(HALF), values)).astype(HALF)
-
-
-def pair_back(weights, queries, keys, values, upstream):
+def pair_forward(rounded, values):
+    return one_pair(dot_tn(rounded, values)).astype(HALF)
+
+
+def pair_back(weights, rounded, queries, keys, values, upstream):
     weight_grad = dot_nt(values, upstream)
     inner = jnp.sum(weights * weight_grad, axis=0, keepdims=True)
     score_grad = (weights * (weight_grad - inner) * 0.125).astype(HALF)
     query_grad = one_pair(dot_tn(score_grad, keys)).astype(HALF)
     key_grad = dot(score_grad, queries).astype(HALF)
-    value_grad = dot(weights.astype(HALF), upstream).astype(HALF)
+    value_grad = dot(rounded, upstream).astype(HALF)
     return query_grad, key_grad, value_grad
 
 
@@ -273,7 +277,7 @@
         for matrix in ("_pack", "_own", "_halo"):
             setattr(r, kind + matrix, getattr(r, held + matrix))
     r.patches_grad = r.fine_out
-    for name in LOADED[:11]:
+    for name in LOADED[:6]:
         load(name)
 
     barrier = pltpu.get_barrier_semaphore()
@@ -341,8 +345,10 @@
     needs = ((), (LON,), (LAT,), (LON, LAT, DIAG))
     waited = set()
     mid_arrive = []
-    for name in ("in_own", "in_halo", "qkv_f", "proj_f", "mid_pack"):
+    for name in LOADED[1:6]:
         loads[name].wait()
+    for name in LOADED[6:11]:
+        load(name)
     for w in range(4):
         for slot in needs[w]:
             if slot not in waited:
@@ -363,8 +369,10 @@
             at = 128 * p
             queries = two_heads(qkv[rows, at : at + 128])
             weights = pair_weights(queries, qkv[rows, 512 + at : 640 + at], mask)
+            rounded = weights.astype(HALF)
+            r.kept[4 * w + p] = rounded
             r.attended[rows, at : at + 128] = pair_forward(
-                weights, qkv[rows, 1024 + at : 1152 + at]
+                rounded, qkv[rows, 1024 + at : 1152 + at]
             )
         attended = r.attended[rows, :]
         split(attended, keep4, give4, "attended", rows)
@@ -427,9 +435,10 @@
         queries = two_heads(qkv[:, at : at + 128])
         keys, worth = qkv[:, 1024 + at : 1152 + at], qkv[:, 2048 + at : 2176 + at]
         weights = pair_weights(queries, keys, mask)
-        r.coarse_attended[:, at : at + 128] = pair_forward(weights, worth)
+        rounded = weights.astype(HALF)
+        r.coarse_attended[:, at : at + 128] = pair_forward(rounded, worth)
         upstream = two_heads(r.cot_attended[:, at : at + 128])
-        grads = pair_back(weights, queries, keys, worth, upstream)
+        grads = pair_back(weights, rounded, queries, keys, worth, upstream)
         for n in range(3):
             r.qkv_right[own, 1024 * n + at : 1024 * n + at + 128] = grads[n]
     handed_coarse.append(hand_right("qkv_right", 0, CELLS))
@@ -465,56 +474,94 @@
 
     sums = {}
 
-    def start_first(p):
-        axis = ORDERS[p % 3][0]
+    def across(axis):
+        mine = place[axis]
+        near, far = mine + 1 - 2 * (mine % 2), 3 - mine
+        return mine, ((near, far), (far, near))
+
+    def there(axis, index):
+        return device_at({**place, axis: index}, core)
+
+    def stage_of(p, stage):
+        landed = of(r, ("landed0_", "landed1_")[stage], p)
+        lead = LEADS[p % 3][stage]
+        size = int(np.prod(lead))
+        if stage == 0:
+            source = lambda index: first_cut(p % 3, of(r, "share", p), index)
+        else:
+            source = lambda index: second_cut(p % 3, of(r, "landed0_", p).at[1], index)
+        return source, landed, lead, size, ORDERS[p % 3][stage]
+
+    def halves(lead):
+        return [pl.ds(h * (lead[0] // 2), lead[0] // 2) for h in range(2)]
+
+    def begin(p, stage):
+        source, landed, lead, size, axis = stage_of(p, stage)
+        mine, pairs = across(axis)
+        sums[p] = {}
+        for slot in range(2):
+            for h, rows in enumerate(halves(lead)):
+                one = pairs[h][0]
+                quarter = lax.rem(mine + 2, 4) if slot == 0 else one
+                sums[p][h, slot] = remote(
+                    source(quarter).at[rows], landed.at[slot, rows], there(axis, one)
+                )
+
+    def forward(p, stage):
+        source, landed, lead, size, axis = stage_of(p, stage)
+        mine, pairs = across(axis)
+        for h, rows in enumerate(halves(lead)):
+            two = pairs[h][1]
+            theirs = source(two)
+            sums[p][h, 0].wait()
+
+            def add(i, carry, h=h, theirs=theirs):
+                at = spots(lead, i + h * (size // 2))
+                landed[(0,) + at] = added(theirs[at], [landed[(0,) + at]]).astype(HALF)
+                return carry
+
+            lax.fori_loop(0, size // 2, add, 0)
+            sums[p][h, 2] = remote(landed.at[0, rows], landed.at[2, rows], there(axis, two))
+
+    def collect(p, stage):
+        source, landed, lead, size, axis = stage_of(p, stage)
+        mine = source(place[axis])
+        for h in range(2):
+            sums[p][h, 1].wait()
+            sums[p][h, 2].wait()
+
+        def add(i, carry):
+            at = spots(lead, i)
+            total = added(mine[at], [landed[(1,) + at], landed[(2,) + at]])
+            landed[(1,) + at] = total.astype(HALF)
+            return carry
+
+        lax.fori_loop(0, size, add, 0)
+
+    def start_second(p):
+        source, landed, lead, size, axis = stage_of(p, 1)
         sums[p] = []
         for k in (2, 1, 3):
             moved = along(place, axis, k)
             sums[p].append(
-                remote(
-                    first_cut(p % 3, of(r, "share", p), moved[axis]),
-                    of(r, "landed0_", p).at[k - 1],
-                    device_at(moved, core),
-                )
+                remote(source(moved[axis]), landed.at[k - 1], device_at(moved, core))
             )
 
-    def start_second(p):
+    def collect_second(p):
+        source, landed, lead, size, axis = stage_of(p, 1)
         for copy in sums[p]:
             copy.wait()
-        mine = first_cut(p % 3, of(r, "share", p), place[ORDERS[p % 3][0]])
-
-        def add(i, carry):
-            at = spots(LEADS[p % 3][0], i)
-            total = added(mine[at], [of(r, "landed0_", p)[(k,) + at] for k in range(3)])
-            of(r, "landed0_", p)[(0,) + at] = total.astype(HALF)
-            return carry
-
-        lax.fori_loop(0, 16, add, 0)
-        axis = ORDERS[p % 3][1]
-        sums[p] = []
-        for k in (2, 1, 3):
-            moved = along(place, axis, k)
-            sums[p].append(
-                remote(
-                    second_cut(p % 3, of(r, "landed0_", p).at[0], moved[axis]),
-                    of(r, "landed1_", p).at[k - 1],
-                    device_at(moved, core),
-                )
-            )
+        total = added(source(place[axis])[...], [landed[k] for k in range(3)])
+        landed[1] = total.astype(HALF)
 
     def start_third(p):
-        for copy in sums[p]:
-            copy.wait()
-        mine = second_cut(p % 3, of(r, "landed0_", p).at[0], place[ORDERS[p % 3][1]])
-        total = added(mine[...], [of(r, "landed1_", p)[k] for k in range(3)])
-        of(r, "summed1_", p)[...] = total.astype(HALF)
         axis = ORDERS[p % 3][2]
         sums[p] = []
         for k in (2, 1, 3):
             moved = along(place, axis, k)
             sums[p].append(
                 remote(
-                    third_cut(p % 3, of(r, "summed1_", p), moved[axis]),
+                    third_cut(p % 3, of(r, "landed1_", p).at[1], moved[axis]),
                     of(r, "landed2_", p).at[k - 1],
                     device_at(moved, core),
                 )
@@ -523,7 +570,7 @@
     def finish(p):
         for copy in sums[p]:
             copy.wait()
-        mine = third_cut(p % 3, of(r, "summed1_", p), place[ORDERS[p % 3][2]])
+        mine = third_cut(p % 3, of(r, "landed1_", p).at[1], place[ORDERS[p % 3][2]])
         total = added(mine[...], [of(r, "landed2_", p)[k] for k in range(3)])
         of(r, "sum", p)[...] = total
 
@@ -556,8 +603,8 @@
 
     lax.fori_loop(0, 2, qkv_rows, 0)
     if summing:
-        start_first(1)
-        start_first(2)
+        begin(1, 0)
+        begin(2, 0)
     for copy in gains_handed + [merged_handed, inner_handed]:
         copy.wait()
     ones = jnp.ones((32, 128), HALF)
@@ -576,7 +623,7 @@
 
     lax.fori_loop(0, 4, merge_rows, 0)
     if summing:
-        start_first(0)
+        begin(0, 0)
 
     needs = ((LON, LAT, DIAG), (LAT,), (LON,), ())
     waited = set()
@@ -593,14 +640,13 @@
         handed_fine.append(hand_right("fine_right", CELLS * w, CELLS))
         attended_grad = dot_nt(grad, r.proj_f[...]).astype(HALF)
         qkv = r.qkv
-        mask = pair_mask(edge if w >= 2 else 0)
         for p in range(4):
             at = 128 * p
             queries = two_heads(qkv[rows, at : at + 128])
             keys, worth = qkv[rows, 512 + at : 640 + at], qkv[rows, 1024 + at : 1152 + at]
-            weights = pair_weights(queries, keys, mask)
+            rounded = r.kept[4 * w + p]
             upstream = two_heads(attended_grad[:, at : at + 128])
-            grads = pair_back(weights, queries, keys, worth, upstream)
+            grads = pair_back(rounded.astype(FULL), rounded, queries, keys, worth, upstream)
             for n in range(3):
                 r.triple_right[rows, 512 * n + at : 512 * n + at + 128] = grads[n]
         handed_fine.append(hand_right("triple_right", CELLS * w, CELLS))
@@ -614,8 +660,15 @@
                 loads["end_pack"].wait()
             pack_piece("end", r.tokens_back[...], slot, fine_sizes[slot])
             end_arrive.append(send_piece("end", slot, fine_sizes[slot], -1))
+        if summing:
+            for p in {3: (1, 2), 2: (0,)}.get(w, ()):
+                forward(p, 0)
     split(in_two(gain_row), keep4, give4, "gain_fine", slice(0, 16))
     handed_fine.append(hand_left("gain_fine"))
+    if summing:
+        for p in (1, 2):
+            collect(p, 0)
+            begin(p, 1)
     for copy in handed_fine:
         copy.wait()
 
@@ -640,26 +693,38 @@
     lax.fori_loop(0, 2, fine_rows, 0)
     if summing:
         for p in (3, 4, 5):
-            start_first(p)
-        for p in (1, 2, 0):
-            start_second(p)
+            begin(p, 0)
+        collect(0, 0)
+        begin(0, 1)
+        forward(1, 1)
+        forward(2, 1)
     for copy in out_arrive:
         copy.wait()
-    for name in ("end_own", "end_halo"):
-        loads[name].wait()
     r.coarse_tokens[...] = gathered(
         "out", every, r.coarse_out[...], coarse_sizes, (LON, LAT, DIAG)
     ).astype(HALF)
     if summing:
         for p in (3, 4, 5):
-            start_second(p)
+            forward(p, 0)
+        forward(0, 1)
+    for name in ("end_own", "end_halo"):
+        loads[name].wait()
     for copy in end_arrive:
         copy.wait()
     r.tokens_grad[...] = gathered(
         "end", every, r.tokens_back[...], fine_sizes, (LON, LAT, DIAG)
     ).astype(HALF)
     if summing:
-        for p in (1, 2, 0, 3, 4, 5):
+        for p in (1, 2):
+            collect(p, 1)
+            start_third(p)
+        for p in (3, 4, 5):
+            collect(p, 0)
+            start_second(p)
+        collect(0, 1)
+        start_third(0)
+        for p in (3, 4, 5):
+            collect_second(p)
             start_third(p)
         for p in (1, 2, 0, 3, 4, 5):
             finish(p)
@@ -704,11 +769,11 @@
 
     values = dict(values)
     values.update(matrices("in", 12, 24, "natural", "window", 1))
-    values.update(matrices("cot", 6, 12, "natural", "window", 1))
+    values.update(matrices("cot", 6, 12, "last", "window", 1))
     values.update(matrices("mid", 12, 24, "window", "patch", 1))
     values.update(matrices("back", 12, 24, "patch", "window", -1))
     values.update(matrices("end", 12, 24, "window", "natural", -1))
-    values.update(matrices("out", 6, 12, "window", "natural", -1))
+    values.update(matrices("out", 6, 12, "window", "last", -1))
     specs, operands = [], []
     for name, value in values.items():
         loaded = name in LOADED
@@ -732,6 +797,7 @@
         half[name + "_left"] = (2 * count, width)
         half[name + "_give"] = (count, width)
     half.update(
+        kept=(16, CELLS, 2 * CELLS),
         rolled=(576, 512),
         qkv=(576, 1536),
         attended=(576, 512),
@@ -754,12 +820,11 @@
             half["landed0_" + str(p)] = (3,) + first + (16, width)
             half["landed1_" + str(p)] = (3,) + second + (16, width)
             half["landed2_" + str(p)] = (3, 16, width)
-            half["summed1_" + str(p)] = second + (16, width)
     memory = {name: pltpu.VMEM(shape, HALF) for name, shape in half.items()}
     memory["unit_merge"] = pltpu.VMEM((CELLS, 2048), FULL)
     memory["unit_coarse"] = pltpu.VMEM((CELLS, 1024), FULL)
-    memory["send_sem"] = pltpu.SemaphoreType.DMA((100,))
-    memory["recv_sem"] = pltpu.SemaphoreType.DMA((100,))
+    memory["send_sem"] = pltpu.SemaphoreType.DMA((150,))
+    memory["recv_sem"] = pltpu.SemaphoreType.DMA((150,))
     memory["load_sem"] = pltpu.SemaphoreType.DMA((len(LOADED),))
     outputs = {
         "coarse_tokens": jax.ShapeDtypeStruct((CELLS, 1024), HALF),
@@ -799,7 +864,7 @@
 ):
     return dict(
         tokens=tokens.reshape(576, 512),
-        cotangent=cotangent.reshape(CELLS, 1024),
+        cotangent=cotangent.transpose(1, 2, 0, 3).reshape(CELLS, 1024),
         gain_f=gain_fine.reshape(1, 512),
         gain_m=gain_merge.reshape(1, 2048),
         gain_c=gain_coarse.reshape(1, 1024),
@@ -859,7 +924,7 @@
         last_kernel, out_shape=shapes, in_specs=[VMEM] * 8, out_specs=[VMEM] * 10
     )(*found)
     outs = list(outs)
-    outs[0] = outs[0].reshape(2, 6, 12, 1024)
+    outs[0] = outs[0].reshape(6, 12, 2, 1024).transpose(2, 0, 1, 3)
     outs[1] = outs[1].reshape(2, 12, 24, 512)
     for n in (2, 5, 7):
         outs[n] = outs[n].reshape(-1)

time: 103 us -> 101 us (0.981)
  Pallas kernels: 98.4 us -> 96.3 us
    pallas_call x1, Pallas kernels: 96.2 us -> 94.1 us  [whole(): pl.pallas_call(functools.partial(whole_kernel, names, summing), out_shape...]
    unnamed x2 -> x0, local copies, waits for them, and re-layouts: 2.05 us -> none
    reshape x2, local copies, waits for them, and re-layouts: 1.81 us -> 3.57 us  [the longest x1 1.79 us: last(): outs[0] = outs[0].reshape(6, 12, 2, 1024).transpose(2, 0, 1, 3)]
where the time goes in v3:
time: 101 us
  Pallas kernels  96.3 us (95%)
  local copies, waits for them, and re-layouts  3.57 us (4%)
    pallas_call x1, Pallas kernels, whole(): pl.pallas_call(functools.partial(whole_kernel, names, summing), out_shape...  94.1 us
    pallas_call x1, Pallas kernels, last(): pl.pallas_call(last_kernel, out_shape=shapes, in_specs=[VMEM] * 8, out_sp...  2.27 us

profile of v3, /device:TPU:0, one launch (start us, length us, event | category | flops | bytes accessed | tf_op | source)
XLA Modules:
  0.0 100.6 jit_solution(12173514978733432081)
XLA Ops:
  0.6 1.8 %reshape.51.refs_1_ = bf16[144,1024]{1,0:T(8,128)(2,1)} reshape(bf16[6,12,2,1024]{3,2,1,0:T(2,128)(2,1)} %bitcast.11) | data formatting | bytes 589824 | tf_op jit(solution)/shard_map/reshape | solution.py:867
  2.4 94.1 %shard_map.339 = (bf16[144,1024]{1,0:T(8,128)(2,1)}, bf16[576,512]{1,0:T(8,128)(2,1)}, f32[16,1152]{1,0:T(8,128)}, f32[16,1024]{1,0:T(8,128)}, f32[16,1024]{1,0:...) custom-call(bf16[576,512]{1,0:T(8,128)(2,1)} %bitcast.10, bf16[144,1024]{1,0:T(8,128)(2,1)} %reshape.51.refs_1_, ...), custom_call_target="tpu_custom_call" | custom-call | tf_op jit(solution)/shard_map/pallas_call | solution.py:840
  96.5 2.3 %shard_map.340 = (bf16[144,1024]{1,0:T(8,128)(2,1)}, bf16[576,512]{1,0:T(8,128)(2,1)}, f32[1,4]{1,0:T(1,128)}, f32[4,1536]{1,0:T(4,128)}, f32[4,512]{1,0:T(4,128...) custom-call(bf16[144,1024]{1,0:T(8,128)(2,1)} %get-tuple-element.28.ref, ...), custom_call_target="tpu_custom_call" | custom-call | tf_op jit(solution)/shard_map/pallas_call | solution.py:923
  98.8 1.8 %reshape.55 = bf16[6,12,2,1024]{3,2,1,0:T(2,128)(2,1)} reshape(bf16[144,1024]{1,0:T(8,128)(2,1)} %get-tuple-element.36) | data formatting | bytes 589824 | tf_op jit(solution)/shard_map/reshape | solution.py:927

commit v4 on v3

--- a/solution.py
+++ b/solution.py
@@ -277,6 +277,7 @@
         for matrix in ("_pack", "_own", "_halo"):
             setattr(r, kind + matrix, getattr(r, held + matrix))
     r.patches_grad = r.fine_out
+    r.normal, r.cot_flat, r.wide = r.tokens_back, r.coarse_attended, r.unit_coarse
     for name in LOADED[:6]:
         load(name)
 
@@ -312,13 +313,15 @@
     loads["in_pack"].wait()
     for slot in (LAT, DIAG, LON):
         pack_piece("in", r.tokens[...], slot, fine_sizes[slot])
-    for slot in (LAT, DIAG, LON):
-        pack_piece("cot", r.cotangent[...], slot, coarse_sizes[slot])
     pl.semaphore_wait(barrier, len(partners))
     arrive = {slot: send_piece("in", slot, fine_sizes[slot], 1) for slot in (LAT, DIAG, LON)}
-    cot_arrive = [send_piece("cot", slot, coarse_sizes[slot], 1) for slot in (LAT, DIAG, LON)]
+    for n in range(12):
+        r.wide[WW * n : WW * n + WW, :] = r.cotangent[n // 6, n % 6].astype(FULL)
+    cotangent = r.wide[...].astype(HALF)
+    r.cot_flat[...] = cotangent
+    for slot in (LAT, DIAG, LON):
+        pack_piece("cot", cotangent, slot, coarse_sizes[slot])
     r.fine_out[...] = jnp.zeros_like(r.fine_out)
-    r.tokens_back[...] = jnp.zeros_like(r.tokens_back)
 
     keep4, give4 = owner_pick(4, core), owner_pick(4, 1 - core)
     keep8, give8 = owner_pick(8, core), owner_pick(8, 1 - core)
@@ -359,7 +362,7 @@
         r.rolled[rows, :] = values.astype(HALF)
         unit, _ = norm_parts(values)
         normed = (unit * r.gain_f[...]).astype(HALF)
-        split(normed, keep4, give4, "normal", rows)
+        r.normal[rows, :] = normed
         qkv = r.qkv
         for n in range(3):
             cols = slice(512 * n, 512 * n + 512)
@@ -375,24 +378,21 @@
                 rounded, qkv[rows, 1024 + at : 1152 + at]
             )
         attended = r.attended[rows, :]
-        split(attended, keep4, give4, "attended", rows)
         r.fine_out[rows, :] = (values + dot(attended, r.proj_f[...])).astype(HALF)
         for slot in {1: (LAT,), 2: (DIAG, LON)}.get(w, ()):
             pack_piece("mid", r.fine_out[...], slot, fine_sizes[slot])
             mid_arrive.append(send_piece("mid", slot, fine_sizes[slot], 1))
+        if w == 2:
+            cot_arrive = [send_piece("cot", n, coarse_sizes[n], 1) for n in (LAT, DIAG, LON)]
+    for w in range(4):
+        rows = slice(CELLS * w, CELLS * w + CELLS)
+        split(r.normal[rows, :], keep4, give4, "normal", rows)
+        split(r.attended[rows, :], keep4, give4, "attended", rows)
     handed_fine += [hand_left("normal"), hand_left("attended")]
     for name in LOADED[11:14]:
         load(name)
 
-    for copy in cot_arrive:
-        copy.wait()
-    every = slice(None)
-    cot = gathered("cot", every, r.cotangent[...], coarse_sizes, (LON, LAT, DIAG)).astype(HALF)
-    own = slice(0, CELLS)
-    r.cot_right[own, :] = cot
-    handed_coarse.append(hand_right("cot_right", 0, CELLS))
-    loads["proj_c"].wait()
-    r.cot_attended[...] = dot_nt(cot, r.proj_c[...]).astype(HALF)
+    every, own = slice(None), slice(0, CELLS)
     loads["mid_own"].wait()
     loads["mid_halo"].wait()
     for copy in mid_arrive:
@@ -428,6 +428,13 @@
         r.qkv_coarse[:, cols] = dot(normed, r.qkv_c[:, cols]).astype(HALF)
     split(normed, keep8, give8, "normed", own)
     handed_coarse.append(hand_left("normed"))
+    for copy in cot_arrive:
+        copy.wait()
+    cot = gathered("cot", every, r.cot_flat[...], coarse_sizes, (LON, LAT, DIAG)).astype(HALF)
+    r.cot_right[own, :] = cot
+    handed_coarse.append(hand_right("cot_right", 0, CELLS))
+    loads["proj_c"].wait()
+    r.cot_attended[...] = dot_nt(cot, r.proj_c[...]).astype(HALF)
     qkv = r.qkv_coarse
     mask = pair_mask(edge)
     for p in range(8):
@@ -470,7 +477,6 @@
     r.coarse_out[...] = (coarse_in + dot(attended, r.proj_c[...])).astype(HALF)
     for slot in (LAT, DIAG, LON):
         pack_piece("out", r.coarse_out[...], slot, coarse_sizes[slot])
-    out_arrive = [send_piece("out", slot, coarse_sizes[slot], -1) for slot in (LAT, DIAG, LON)]
 
     sums = {}
 
@@ -520,7 +526,7 @@
                 landed[(0,) + at] = added(theirs[at], [landed[(0,) + at]]).astype(HALF)
                 return carry
 
-            lax.fori_loop(0, size // 2, add, 0)
+            lax.fori_loop(0, size // 2, add, 0, unroll=2)
             sums[p][h, 2] = remote(landed.at[0, rows], landed.at[2, rows], there(axis, two))
 
     def collect(p, stage):
@@ -536,7 +542,34 @@
             landed[(1,) + at] = total.astype(HALF)
             return carry
 
-        lax.fori_loop(0, size, add, 0)
+        lax.fori_loop(0, size, add, 0, unroll=4)
+
+    def start_first(p):
+        axis = ORDERS[p % 3][0]
+        sums[p] = []
+        for k in (2, 1, 3):
+            moved = along(place, axis, k)
+            sums[p].append(
+                remote(
+                    first_cut(p % 3, of(r, "share", p), moved[axis]),
+                    of(r, "landed0_", p).at[k - 1],
+                    device_at(moved, core),
+                )
+            )
+
+    def collect_first(p):
+        source, landed, lead, size, axis = stage_of(p, 0)
+        mine = source(place[axis])
+        for copy in sums[p]:
+            copy.wait()
+
+        def add(i, carry):
+            at = spots(lead, i)
+            total = added(mine[at], [landed[(k,) + at] for k in range(3)])
+            landed[(1,) + at] = total.astype(HALF)
+            return carry
+
+        lax.fori_loop(0, size, add, 0, unroll=4)
 
     def start_second(p):
         source, landed, lead, size, axis = stage_of(p, 1)
@@ -628,7 +661,6 @@
     needs = ((LON, LAT, DIAG), (LAT,), (LON,), ())
     waited = set()
     end_arrive = []
-    gain_row = jnp.zeros((1, 512), FULL)
     for w in (3, 2, 1, 0):
         for slot in needs[w]:
             if slot not in waited:
@@ -650,63 +682,85 @@
             for n in range(3):
                 r.triple_right[rows, 512 * n + at : 512 * n + at + 128] = grads[n]
         handed_fine.append(hand_right("triple_right", CELLS * w, CELLS))
+        if w == 3:
+            out_arrive = [send_piece("out", n, coarse_sizes[n], -1) for n in (LAT, DIAG, LON)]
+        if summing:
+            for p in {2: (1, 2), 0: (0,)}.get(w, ()):
+                forward(p, 0)
+    for copy in handed_fine:
+        copy.wait()
+
+    def store(n, p, at, pieces):
+        width = pieces[0].shape[1]
+        for side, value in enumerate(four_stacked(pieces)):
+            of(r, "share", p)[pl.ds(n * 2, 2), :, :, side, :, at : at + width] = value.reshape(
+                2, 2, 4, 16, width
+            )
+
+    def fine_rows(n, carry):
+        cols = pl.ds(pl.multiple_of(n * 128, 128), 128)
+        grad = dot_tn(r.normal_left[:, cols], r.triple_right[...])
+        store(n, 3, 0, [grad[:, 384 * m : 384 * m + 256] for m in range(4)])
+        store(n, 4, 0, [grad[:, 384 * m + 256 : 384 * m + 384] for m in range(4)])
+        grad = dot_tn(r.attended_left[:, cols], r.fine_right[...])
+        store(n, 4, 128, [grad[:, 128 * m : 128 * m + 128] for m in range(4)])
+        return carry
+
+    lax.fori_loop(0, 2, fine_rows, 0)
+    if summing:
+        for p in (3, 4):
+            start_first(p)
+        for p in (1, 2):
+            collect(p, 0)
+            begin(p, 1)
+    gain_row = jnp.zeros((1, 512), FULL)
+    r.tokens_back[...] = jnp.zeros_like(r.tokens_back)
+    for w in (3, 2, 1, 0):
+        rows = slice(CELLS * w, CELLS * w + CELLS)
         normed_grad = dot_nt(r.triple_right[rows, :], r.qkv_f[...]).astype(HALF).astype(FULL)
         unit, scale = norm_parts(r.rolled[rows, :].astype(FULL))
         gain_row = gain_row + jnp.sum(normed_grad * unit, axis=0, keepdims=True)
         back = norm_back(normed_grad, unit, scale, r.gain_f[...])
-        r.tokens_back[rows, :] = (grad.astype(FULL) + back).astype(HALF)
+        r.tokens_back[rows, :] = (r.fine_right[rows, :].astype(FULL) + back).astype(HALF)
         for slot in {2: (LAT,), 1: (DIAG, LON)}.get(w, ()):
             if not end_arrive:
                 loads["end_pack"].wait()
             pack_piece("end", r.tokens_back[...], slot, fine_sizes[slot])
             end_arrive.append(send_piece("end", slot, fine_sizes[slot], -1))
-        if summing:
-            for p in {3: (1, 2), 2: (0,)}.get(w, ()):
-                forward(p, 0)
+        if summing and w == 2:
+            collect(0, 0)
+            begin(0, 1)
+            forward(1, 1)
+            forward(2, 1)
     split(in_two(gain_row), keep4, give4, "gain_fine", slice(0, 16))
-    handed_fine.append(hand_left("gain_fine"))
+    gain_handed = hand_left("gain_fine")
     if summing:
-        for p in (1, 2):
-            collect(p, 0)
-            begin(p, 1)
-    for copy in handed_fine:
-        copy.wait()
-
-    def fine_rows(n, carry):
-        cols = pl.ds(pl.multiple_of(n * 128, 128), 128)
-
-        def store(p, at, pieces):
-            width = pieces[0].shape[1]
-            for side, value in enumerate(four_stacked(pieces)):
-                of(r, "share", p)[pl.ds(n * 2, 2), :, :, side, :, at : at + width] = value.reshape(
-                    2, 2, 4, 16, width
-                )
-
-        grad = dot_tn(r.normal_left[:, cols], r.triple_right[...])
-        store(3, 0, [grad[:, 384 * m : 384 * m + 256] for m in range(4)])
-        store(4, 0, [grad[:, 384 * m + 256 : 384 * m + 384] for m in range(4)])
-        grad = dot_tn(r.attended_left[:, cols], r.fine_right[...])
-        store(4, 128, [grad[:, 128 * m : 128 * m + 128] for m in range(4)])
-        store(5, 0, [dot_tn(r.gain_fine_left[:, cols], ones)] * 4)
-        return carry
-
-    lax.fori_loop(0, 2, fine_rows, 0)
+        for p in (3, 4):
+            collect_first(p)
+            start_second(p)
+        forward(0, 1)
+    gain_handed.wait()
+    for n in range(2):
+        cols = slice(128 * n, 128 * n + 128)
+        store(n, 5, 0, [dot_tn(r.gain_fine_left[:, cols], ones)] * 4)
     if summing:
-        for p in (3, 4, 5):
-            begin(p, 0)
-        collect(0, 0)
-        begin(0, 1)
-        forward(1, 1)
-        forward(2, 1)
+        start_first(5)
     for copy in out_arrive:
         copy.wait()
     r.coarse_tokens[...] = gathered(
         "out", every, r.coarse_out[...], coarse_sizes, (LON, LAT, DIAG)
     ).astype(HALF)
     if summing:
-        for p in (3, 4, 5):
-            forward(p, 0)
-        forward(0, 1)
+        for p in (1, 2):
+            collect(p, 1)
+            start_third(p)
+        collect_first(5)
+        start_second(5)
+        for p in (3, 4):
+            collect_second(p)
+            start_third(p)
+        collect(0, 1)
+        start_third(0)
     for name in ("end_own", "end_halo"):
         loads[name].wait()
     for copy in end_arrive:
@@ -715,17 +769,8 @@
         "end", every, r.tokens_back[...], fine_sizes, (LON, LAT, DIAG)
     ).astype(HALF)
     if summing:
-        for p in (1, 2):
-            collect(p, 1)
-            start_third(p)
-        for p in (3, 4, 5):
-            collect(p, 0)
-            start_second(p)
-        collect(0, 1)
-        start_third(0)
-        for p in (3, 4, 5):
-            collect_second(p)
-            start_third(p)
+        collect_second(5)
+        start_third(5)
         for p in (1, 2, 0, 3, 4, 5):
             finish(p)
     else:
@@ -769,11 +814,11 @@
 
     values = dict(values)
     values.update(matrices("in", 12, 24, "natural", "window", 1))
-    values.update(matrices("cot", 6, 12, "last", "window", 1))
+    values.update(matrices("cot", 6, 12, "natural", "window", 1))
     values.update(matrices("mid", 12, 24, "window", "patch", 1))
     values.update(matrices("back", 12, 24, "patch", "window", -1))
     values.update(matrices("end", 12, 24, "window", "natural", -1))
-    values.update(matrices("out", 6, 12, "window", "last", -1))
+    values.update(matrices("out", 6, 12, "window", "natural", -1))
     specs, operands = [], []
     for name, value in values.items():
         loaded = name in LOADED
@@ -864,7 +909,7 @@
 ):
     return dict(
         tokens=tokens.reshape(576, 512),
-        cotangent=cotangent.transpose(1, 2, 0, 3).reshape(CELLS, 1024),
+        cotangent=cotangent,
         gain_f=gain_fine.reshape(1, 512),
         gain_m=gain_merge.reshape(1, 2048),
         gain_c=gain_coarse.reshape(1, 1024),
@@ -879,7 +924,9 @@
 def last_kernel(*refs):
     coarse, tokens, a, b, c, d, e, f = refs[:8]
     coarse_out, tokens_out, fine_gain, qkv_f, proj_f, merge_gain, merge, coarse_gain, qkv_c, proj_c = refs[8:]
-    coarse_out[...] = coarse[...]
+    cells = coarse[...].astype(FULL)
+    for n in range(12):
+        coarse_out[n // 6, n % 6] = cells[WW * n : WW * n + WW].astype(HALF)
     tokens_out[...] = tokens[...]
 
     def across(column, count):
@@ -906,7 +953,7 @@
 
 
 def last(found):
-    shapes = [jax.ShapeDtypeStruct((CELLS, 1024), HALF), jax.ShapeDtypeStruct((576, 512), HALF)]
+    shapes = [jax.ShapeDtypeStruct((2, 6, WW, 1024), HALF), jax.ShapeDtypeStruct((576, 512), HALF)]
     shapes += [
         jax.ShapeDtypeStruct(shape, FULL)
         for shape in (
@@ -924,7 +971,6 @@
         last_kernel, out_shape=shapes, in_specs=[VMEM] * 8, out_specs=[VMEM] * 10
     )(*found)
     outs = list(outs)
-    outs[0] = outs[0].reshape(6, 12, 2, 1024).transpose(2, 0, 1, 3)
     outs[1] = outs[1].reshape(2, 12, 24, 512)
     for n in (2, 5, 7):
         outs[n] = outs[n].reshape(-1)

time: 101 us -> 102 us (level)
  Pallas kernels: 96.3 us -> 97.5 us
    unnamed x0 -> x2, local copies, waits for them, and re-layouts: none -> 3.8 us
    reshape x2 -> x0, local copies, waits for them, and re-layouts: 3.57 us -> none  [the longest x1 1.79 us: last(): outs[0] = outs[0].reshape(6, 12, 2, 1024).transpose(2, 0, 1, 3)]
    pallas_call x1, Pallas kernels: 94.1 us -> 95.2 us  [whole(): pl.pallas_call(functools.partial(whole_kernel, names, summing), out_shape...]
where the time goes in v4:
time: 102 us
  Pallas kernels  97.5 us (96%)
  local copies, waits for them, and re-layouts  3.8 us (4%)
    pallas_call x1, Pallas kernels, whole(): pl.pallas_call(functools.partial(whole_kernel, names, summing), out_shape...  95.2 us
    unnamed x2, local copies, waits for them, and re-layouts  3.8 us
    pallas_call x1, Pallas kernels, last(): pl.pallas_call(last_kernel, out_shape=shapes, in_specs=[VMEM] * 8, out_sp...  2.3 us

profile of v4, /device:TPU:0, one launch (start us, length us, event | category | flops | bytes accessed | tf_op | source)
XLA Modules:
  0.0 102.0 jit_solution(6074219354210921210)
XLA Ops:
  0.6 1.8 %copy.38.refs_1_ = bf16[2,6,12,1024]{3,2,1,0:T(8,128)(2,1)} copy(bf16[2,6,12,1024]{3,0,2,1:T(2,128)(2,1)} %param.29) | data formatting | bytes 589824 | tf_op args[1]
  2.4 95.2 %shard_map.339 = (bf16[144,1024]{1,0:T(8,128)(2,1)}, bf16[576,512]{1,0:T(8,128)(2,1)}, f32[16,1152]{1,0:T(8,128)}, f32[16,1024]{1,0:T(8,128)}, f32[16,1024]{1,0:...) custom-call(bf16[576,512]{1,0:T(8,128)(2,1)} %bitcast.8, ...), custom_call_target="tpu_custom_call" | custom-call | tf_op jit(solution)/shard_map/pallas_call | solution.py:885
  97.7 2.3 %shard_map.340 = (bf16[2,6,12,1024]{3,2,1,0:T(8,128)(2,1)}, bf16[576,512]{1,0:T(8,128)(2,1)}, f32[1,4]{1,0:T(1,128)}, f32[4,1536]{1,0:T(4,128)}, f32[4,512]{1,0:...) custom-call(bf16[144,1024]{1,0:T(8,128)(2,1)} %get-tuple-element.28., ...), custom_call_target="tpu_custom_call" | custom-call | tf_op jit(solution)/shard_map/pallas_call | solution.py:970
  100.0 2.0 %copy.39 = bf16[2,6,12,1024]{3,0,2,1:T(2,128)(2,1)} copy(bf16[2,6,12,1024]{3,2,1,0:T(8,128)(2,1)} %get-tuple-element.46) | data formatting | bytes 589824

commit v5 on v4

--- a/solution.py
+++ b/solution.py
@@ -277,7 +277,9 @@
         for matrix in ("_pack", "_own", "_halo"):
             setattr(r, kind + matrix, getattr(r, held + matrix))
     r.patches_grad = r.fine_out
-    r.normal, r.cot_flat, r.wide = r.tokens_back, r.coarse_attended, r.unit_coarse
+    r.normal, r.wide, r.coarse_in = r.tokens_back, r.unit_coarse, r.coarse_out
+    r.cot_flat = r.inner_right.at[pl.ds(0, CELLS)]
+    r.back_packed, r.end_packed, r.out_packed = r.in_packed, r.mid_packed, r.cot_packed
     for name in LOADED[:6]:
         load(name)
 
@@ -321,7 +323,6 @@
     r.cot_flat[...] = cotangent
     for slot in (LAT, DIAG, LON):
         pack_piece("cot", cotangent, slot, coarse_sizes[slot])
-    r.fine_out[...] = jnp.zeros_like(r.fine_out)
 
     keep4, give4 = owner_pick(4, core), owner_pick(4, 1 - core)
     keep8, give8 = owner_pick(8, core), owner_pick(8, 1 - core)
@@ -343,89 +344,119 @@
         held = getattr(r, name)
         return remote(held.at[pl.ds(start, size)], held.at[pl.ds(half + start, size)], sibling)
 
+    def hand_rows(name, w, base):
+        held = getattr(r, name)
+        half = held.shape[0] // 2
+        start = pl.multiple_of(w * CELLS, 16)
+        return pltpu.make_async_remote_copy(
+            src_ref=held.at[pl.ds(start, CELLS)],
+            dst_ref=held.at[pl.ds(pl.multiple_of(half + w * CELLS, 16), CELLS)],
+            send_sem=r.send_sem.at[base + w],
+            recv_sem=r.recv_sem.at[base + w],
+            device_id=sibling,
+            device_id_type=MESH,
+        )
+
+    def fill(target, left, weight, width):
+        def columns(n, carry):
+            cols = pl.ds(pl.multiple_of(n * width, width), width)
+            target[:, cols] = dot(left(), weight[:, cols]).astype(HALF)
+            return carry
+
+        lax.fori_loop(0, weight.shape[1] // width, columns, 0)
+
+    def fill_nt(target, left, weight, width):
+        def columns(n, carry):
+            cols = pl.ds(pl.multiple_of(n * width, width), width)
+            target[:, cols] = dot_nt(left(), weight[cols, :]).astype(HALF)
+            return carry
+
+        lax.fori_loop(0, weight.shape[0] // width, columns, 0)
+
     handed_fine, handed_coarse, late = [], [], []
 
-    needs = ((), (LON,), (LAT,), (LON, LAT, DIAG))
-    waited = set()
-    mid_arrive = []
+    every, own = slice(None), slice(0, CELLS)
+    all_pieces = (LON, LAT, DIAG)
     for name in LOADED[1:6]:
         loads[name].wait()
     for name in LOADED[6:11]:
         load(name)
-    for w in range(4):
-        for slot in needs[w]:
-            if slot not in waited:
-                arrive[slot].wait()
-                waited.add(slot)
-        rows = slice(CELLS * w, CELLS * w + CELLS)
-        values = gathered("in", rows, r.tokens[...], fine_sizes, needs[w])
+    for slot in all_pieces:
+        arrive[slot].wait()
+
+    def forward_window(w, carry):
+        rows = pl.ds(pl.multiple_of(w * CELLS, 16), CELLS)
+        values = gathered("in", rows, r.tokens[...], fine_sizes, all_pieces)
         r.rolled[rows, :] = values.astype(HALF)
         unit, _ = norm_parts(values)
         normed = (unit * r.gain_f[...]).astype(HALF)
         r.normal[rows, :] = normed
-        qkv = r.qkv
         for n in range(3):
             cols = slice(512 * n, 512 * n + 512)
-            qkv[rows, cols] = dot(normed, r.qkv_f[:, cols]).astype(HALF)
-        mask = pair_mask(edge if w >= 2 else 0)
+            r.qkv[rows, cols] = dot(normed, r.qkv_f[:, cols]).astype(HALF)
+        mask = pair_mask(jnp.where(w >= 2, edge, 0))
         for p in range(4):
             at = 128 * p
-            queries = two_heads(qkv[rows, at : at + 128])
-            weights = pair_weights(queries, qkv[rows, 512 + at : 640 + at], mask)
+            queries = two_heads(r.qkv[rows, at : at + 128])
+            weights = pair_weights(queries, r.qkv[rows, 512 + at : 640 + at], mask)
             rounded = weights.astype(HALF)
             r.kept[4 * w + p] = rounded
             r.attended[rows, at : at + 128] = pair_forward(
-                rounded, qkv[rows, 1024 + at : 1152 + at]
+                rounded, r.qkv[rows, 1024 + at : 1152 + at]
             )
-        attended = r.attended[rows, :]
-        r.fine_out[rows, :] = (values + dot(attended, r.proj_f[...])).astype(HALF)
-        for slot in {1: (LAT,), 2: (DIAG, LON)}.get(w, ()):
-            pack_piece("mid", r.fine_out[...], slot, fine_sizes[slot])
-            mid_arrive.append(send_piece("mid", slot, fine_sizes[slot], 1))
-        if w == 2:
-            cot_arrive = [send_piece("cot", n, coarse_sizes[n], 1) for n in (LAT, DIAG, LON)]
-    for w in range(4):
-        rows = slice(CELLS * w, CELLS * w + CELLS)
+        r.fine_out[rows, :] = (values + dot(r.attended[rows, :], r.proj_f[...])).astype(HALF)
+        return carry
+
+    lax.fori_loop(0, 4, forward_window, 0)
+    mid_arrive = []
+    for slot in (LAT, DIAG, LON):
+        pack_piece("mid", r.fine_out[...], slot, fine_sizes[slot])
+        mid_arrive.append(send_piece("mid", slot, fine_sizes[slot], 1))
+    cot_arrive = [send_piece("cot", n, coarse_sizes[n], 1) for n in (LAT, DIAG, LON)]
+
+    def split_window(w, carry):
+        rows = pl.ds(pl.multiple_of(w * CELLS, 16), CELLS)
         split(r.normal[rows, :], keep4, give4, "normal", rows)
         split(r.attended[rows, :], keep4, give4, "attended", rows)
+        return carry
+
+    lax.fori_loop(0, 4, split_window, 0)
     handed_fine += [hand_left("normal"), hand_left("attended")]
     for name in LOADED[11:14]:
         load(name)
 
-    every, own = slice(None), slice(0, CELLS)
     loads["mid_own"].wait()
     loads["mid_halo"].wait()
     for copy in mid_arrive:
         copy.wait()
-    values = jnp.concatenate(
-        [
-            gathered(
-                "mid",
-                slice(CELLS * g, CELLS * g + CELLS),
-                r.fine_out[...],
-                fine_sizes,
-                (LON, LAT, DIAG),
-            )
-            for g in range(4)
-        ],
-        axis=1,
-    )
+    for g in range(4):
+        rows = slice(CELLS * g, CELLS * g + CELLS)
+        r.merged[:, 512 * g : 512 * g + 512] = gathered(
+            "mid", rows, r.fine_out[...], fine_sizes, all_pieces
+        ).astype(HALF)
     for name in LOADED[14:]:
         load(name)
-    unit, scale_merge = norm_parts(values)
-    r.unit_merge[...] = unit
-    merged = (unit * r.gain_m[...]).astype(HALF)
+
+    def merge_norm(n, carry):
+        rows = pl.ds(pl.multiple_of(n * 48, 16), 48)
+        unit, scale = norm_parts(r.merged[rows, :].astype(FULL))
+        r.unit_merge[rows, :] = unit
+        r.scale_merge[rows, :] = scale
+        r.merged[rows, :] = (unit * r.gain_m[...]).astype(HALF)
+        return carry
+
+    lax.fori_loop(0, 3, merge_norm, 0)
     loads["merge_w"].wait()
-    coarse_in = dot(merged, r.merge_w[...]).astype(HALF).astype(FULL)
-    split(merged, keep16, give16, "merged", own)
+    fill(r.coarse_in, lambda: r.merged[...], r.merge_w, 512)
+    coarse_in = r.coarse_in[...].astype(FULL)
+    split(r.merged[...], keep16, give16, "merged", own)
     merged_handed = hand_left("merged")
     unit, scale_coarse = norm_parts(coarse_in)
     r.unit_coarse[...] = unit
     normed = (unit * r.gain_c[...]).astype(HALF)
+    r.coarse_attended[...] = normed
     loads["qkv_c"].wait()
-    for n in range(3):
-        cols = slice(1024 * n, 1024 * (n + 1))
-        r.qkv_coarse[:, cols] = dot(normed, r.qkv_c[:, cols]).astype(HALF)
+    fill(r.qkv_coarse, lambda: r.coarse_attended[...], r.qkv_c, 512)
     split(normed, keep8, give8, "normed", own)
     handed_coarse.append(hand_left("normed"))
     for copy in cot_arrive:
@@ -437,22 +468,32 @@
     r.cot_attended[...] = dot_nt(cot, r.proj_c[...]).astype(HALF)
     qkv = r.qkv_coarse
     mask = pair_mask(edge)
-    for p in range(8):
-        at = 128 * p
-        queries = two_heads(qkv[:, at : at + 128])
-        keys, worth = qkv[:, 1024 + at : 1152 + at], qkv[:, 2048 + at : 2176 + at]
-        weights = pair_weights(queries, keys, mask)
-        rounded = weights.astype(HALF)
-        r.coarse_attended[:, at : at + 128] = pair_forward(rounded, worth)
-        upstream = two_heads(r.cot_attended[:, at : at + 128])
-        grads = pair_back(weights, rounded, queries, keys, worth, upstream)
-        for n in range(3):
-            r.qkv_right[own, 1024 * n + at : 1024 * n + at + 128] = grads[n]
+
+    def coarse_pairs(n, carry):
+        for side in range(2):
+            start = n * 256 + side * 128
+
+            def part(base):
+                return pl.ds(pl.multiple_of(base + start, 128), 128)
+
+            queries = two_heads(qkv[:, part(0)])
+            keys, worth = qkv[:, part(1024)], qkv[:, part(2048)]
+            weights = pair_weights(queries, keys, mask)
+            rounded = weights.astype(HALF)
+            r.coarse_attended[:, part(0)] = pair_forward(rounded, worth)
+            upstream = two_heads(r.cot_attended[:, part(0)])
+            grads = pair_back(weights, rounded, queries, keys, worth, upstream)
+            for m in range(3):
+                r.qkv_right[own, part(1024 * m)] = grads[m]
+        return carry
+
+    lax.fori_loop(0, 4, coarse_pairs, 0)
     handed_coarse.append(hand_right("qkv_right", 0, CELLS))
     attended = r.coarse_attended[...]
     split(attended, keep8, give8, "coarse", own)
     handed_coarse.append(hand_left("coarse"))
-    normed_grad = dot_nt(r.qkv_right[own, :], r.qkv_c[...]).astype(HALF).astype(FULL)
+    fill_nt(r.cot_attended, lambda: r.qkv_right[own, :], r.qkv_c, 256)
+    normed_grad = r.cot_attended[...].astype(FULL)
     gain_row = jnp.sum(normed_grad * r.unit_coarse[...], axis=0, keepdims=True)
     split(in_two(gain_row), keep8, give8, "gain_coarse", slice(0, 16))
     gains_handed = [hand_left("gain_coarse")]
@@ -461,20 +502,30 @@
     )
     r.inner_right[own, :] = coarse_grad.astype(HALF)
     inner_handed = hand_right("inner_right", 0, CELLS)
-    merged_grad = dot_nt(r.inner_right[own, :], r.merge_w[...]).astype(HALF).astype(FULL)
-    gain_row = jnp.sum(merged_grad * r.unit_merge[...], axis=0, keepdims=True)
+    fill_nt(r.merged, lambda: r.inner_right[own, :], r.merge_w, 512)
+
+    def merge_back(n, gain_row):
+        rows = pl.ds(pl.multiple_of(n * 48, 16), 48)
+        merged_grad = r.merged[rows, :].astype(FULL)
+        unit = r.unit_merge[rows, :]
+        back = norm_back(merged_grad, unit, r.scale_merge[rows, :], r.gain_m[...]).astype(HALF)
+        for g in range(4):
+            place_at = pl.ds(pl.multiple_of(CELLS * g + n * 48, 16), 48)
+            r.patches_grad[place_at, :] = back[:, 512 * g : 512 * (g + 1)]
+        return gain_row + jnp.sum(merged_grad * unit, axis=0, keepdims=True)
+
+    gain_row = lax.fori_loop(0, 3, merge_back, jnp.zeros((1, 2048), FULL))
     split(in_two(gain_row), keep16, give16, "gain_merge", slice(0, 16))
     gains_handed.append(hand_left("gain_merge"))
-    back = norm_back(merged_grad, r.unit_merge[...], scale_merge, r.gain_m[...]).astype(HALF)
-    for g in range(4):
-        r.patches_grad[CELLS * g : CELLS * (g + 1), :] = back[:, 512 * g : 512 * (g + 1)]
     for name in ("back_pack", "back_own", "back_halo"):
         loads[name].wait()
     back_arrive = {}
     for slot in (LAT, DIAG, LON):
         pack_piece("back", r.patches_grad[...], slot, fine_sizes[slot])
         back_arrive[slot] = send_piece("back", slot, fine_sizes[slot], -1)
-    r.coarse_out[...] = (coarse_in + dot(attended, r.proj_c[...])).astype(HALF)
+    r.coarse_out[...] = (
+        r.coarse_in[...].astype(FULL) + dot(r.coarse_attended[...], r.proj_c[...])
+    ).astype(HALF)
     for slot in (LAT, DIAG, LON):
         pack_piece("out", r.coarse_out[...], slot, coarse_sizes[slot])
 
@@ -526,7 +577,7 @@
                 landed[(0,) + at] = added(theirs[at], [landed[(0,) + at]]).astype(HALF)
                 return carry
 
-            lax.fori_loop(0, size // 2, add, 0, unroll=2)
+            lax.fori_loop(0, size // 2, add, 0)
             sums[p][h, 2] = remote(landed.at[0, rows], landed.at[2, rows], there(axis, two))
 
     def collect(p, stage):
@@ -542,7 +593,7 @@
             landed[(1,) + at] = total.astype(HALF)
             return carry
 
-        lax.fori_loop(0, size, add, 0, unroll=4)
+        lax.fori_loop(0, size, add, 0)
 
     def start_first(p):
         axis = ORDERS[p % 3][0]
@@ -569,7 +620,7 @@
             landed[(1,) + at] = total.astype(HALF)
             return carry
 
-        lax.fori_loop(0, size, add, 0, unroll=4)
+        lax.fori_loop(0, size, add, 0)
 
     def start_second(p):
         source, landed, lead, size, axis = stage_of(p, 1)
@@ -658,35 +709,37 @@
     if summing:
         begin(0, 0)
 
-    needs = ((LON, LAT, DIAG), (LAT,), (LON,), ())
-    waited = set()
-    end_arrive = []
-    for w in (3, 2, 1, 0):
-        for slot in needs[w]:
-            if slot not in waited:
-                back_arrive[slot].wait()
-                waited.add(slot)
-        rows = slice(CELLS * w, CELLS * w + CELLS)
-        grad = gathered("back", rows, r.patches_grad[...], fine_sizes, needs[w]).astype(HALF)
+    for slot in all_pieces:
+        back_arrive[slot].wait()
+    fine_base, triple_base = used[0], used[0] + 4
+    used[0] += 8
+
+    def backward_window(w, carry):
+        rows = pl.ds(pl.multiple_of(w * CELLS, 16), CELLS)
+        grad = gathered("back", rows, r.patches_grad[...], fine_sizes, all_pieces).astype(HALF)
         r.fine_right[rows, :] = grad
-        handed_fine.append(hand_right("fine_right", CELLS * w, CELLS))
+        hand_rows("fine_right", w, fine_base).start()
         attended_grad = dot_nt(grad, r.proj_f[...]).astype(HALF)
-        qkv = r.qkv
         for p in range(4):
             at = 128 * p
-            queries = two_heads(qkv[rows, at : at + 128])
-            keys, worth = qkv[rows, 512 + at : 640 + at], qkv[rows, 1024 + at : 1152 + at]
+            queries = two_heads(r.qkv[rows, at : at + 128])
+            keys, worth = r.qkv[rows, 512 + at : 640 + at], r.qkv[rows, 1024 + at : 1152 + at]
             rounded = r.kept[4 * w + p]
             upstream = two_heads(attended_grad[:, at : at + 128])
             grads = pair_back(rounded.astype(FULL), rounded, queries, keys, worth, upstream)
             for n in range(3):
                 r.triple_right[rows, 512 * n + at : 512 * n + at + 128] = grads[n]
-        handed_fine.append(hand_right("triple_right", CELLS * w, CELLS))
-        if w == 3:
-            out_arrive = [send_piece("out", n, coarse_sizes[n], -1) for n in (LAT, DIAG, LON)]
-        if summing:
-            for p in {2: (1, 2), 0: (0,)}.get(w, ()):
-                forward(p, 0)
+        hand_rows("triple_right", w, triple_base).start()
+        return carry
+
+    lax.fori_loop(0, 4, backward_window, 0)
+    out_arrive = [send_piece("out", n, coarse_sizes[n], -1) for n in (LAT, DIAG, LON)]
+    if summing:
+        for p in (1, 2, 0):
+            forward(p, 0)
+    for w in range(4):
+        hand_rows("fine_right", w, fine_base).wait()
+        hand_rows("triple_right", w, triple_base).wait()
     for copy in handed_fine:
         copy.wait()
 
@@ -713,25 +766,26 @@
         for p in (1, 2):
             collect(p, 0)
             begin(p, 1)
-    gain_row = jnp.zeros((1, 512), FULL)
-    r.tokens_back[...] = jnp.zeros_like(r.tokens_back)
-    for w in (3, 2, 1, 0):
-        rows = slice(CELLS * w, CELLS * w + CELLS)
+
+    def norm_window(w, gain_row):
+        rows = pl.ds(pl.multiple_of(w * CELLS, 16), CELLS)
         normed_grad = dot_nt(r.triple_right[rows, :], r.qkv_f[...]).astype(HALF).astype(FULL)
         unit, scale = norm_parts(r.rolled[rows, :].astype(FULL))
-        gain_row = gain_row + jnp.sum(normed_grad * unit, axis=0, keepdims=True)
         back = norm_back(normed_grad, unit, scale, r.gain_f[...])
         r.tokens_back[rows, :] = (r.fine_right[rows, :].astype(FULL) + back).astype(HALF)
-        for slot in {2: (LAT,), 1: (DIAG, LON)}.get(w, ()):
-            if not end_arrive:
-                loads["end_pack"].wait()
-            pack_piece("end", r.tokens_back[...], slot, fine_sizes[slot])
-            end_arrive.append(send_piece("end", slot, fine_sizes[slot], -1))
-        if summing and w == 2:
-            collect(0, 0)
-            begin(0, 1)
-            forward(1, 1)
-            forward(2, 1)
+        return gain_row + jnp.sum(normed_grad * unit, axis=0, keepdims=True)
+
+    gain_row = lax.fori_loop(0, 4, norm_window, jnp.zeros((1, 512), FULL))
+    loads["end_pack"].wait()
+    end_arrive = []
+    for slot in (LAT, DIAG, LON):
+        pack_piece("end", r.tokens_back[...], slot, fine_sizes[slot])
+        end_arrive.append(send_piece("end", slot, fine_sizes[slot], -1))
+    if summing:
+        collect(0, 0)
+        begin(0, 1)
+        forward(1, 1)
+        forward(2, 1)
     split(in_two(gain_row), keep4, give4, "gain_fine", slice(0, 16))
     gain_handed = hand_left("gain_fine")
     if summing:
@@ -827,7 +881,8 @@
         operands.append(value)
     half = {name: values[name].shape for name in LOADED[:11]}
     for kind, width in (("in", 512), ("cot", 1024), ("mid", 512), ("back", 512), ("end", 512), ("out", 1024)):
-        half[kind + "_packed"] = half[kind + "_landed"] = (PACKED, width)
+        half[kind + "_landed"] = (PACKED, width)
+    half.update(in_packed=(PACKED, 512), cot_packed=(PACKED, 1024), mid_packed=(PACKED, 512))
     lefts = dict(
         normal=(576, 256),
         attended=(576, 256),
@@ -853,6 +908,7 @@
         qkv_coarse=(CELLS, 3072),
         coarse_attended=(CELLS, 1024),
         coarse_out=(CELLS, 1024),
+        merged=(CELLS, 2048),
         qkv_right=(2 * CELLS, 3072),
         inner_right=(2 * CELLS, 1024),
         fine_right=(1152, 512),
@@ -867,6 +923,7 @@
             half["landed2_" + str(p)] = (3, 16, width)
     memory = {name: pltpu.VMEM(shape, HALF) for name, shape in half.items()}
     memory["unit_merge"] = pltpu.VMEM((CELLS, 2048), FULL)
+    memory["scale_merge"] = pltpu.VMEM((CELLS, 1), FULL)
     memory["unit_coarse"] = pltpu.VMEM((CELLS, 1024), FULL)
     memory["send_sem"] = pltpu.SemaphoreType.DMA((150,))
     memory["recv_sem"] = pltpu.SemaphoreType.DMA((150,))

time: 102 us -> 116 us (1.14)
  Pallas kernels: 97.5 us -> 111 us
    pallas_call x1, Pallas kernels: 95.2 us -> 109 us  [whole(): pl.pallas_call(functools.partial(whole_kernel, names, summing), out_shape...]
where the time goes in v5:
time: 116 us; the launch traced here: 115 us
  Pallas kernels  111 us (96%)
  local copies, waits for them, and re-layouts  3.8 us (3%)
    pallas_call x1, Pallas kernels, whole(): pl.pallas_call(functools.partial(whole_kernel, names, summing), out_shape...  109 us
    unnamed x2, local copies, waits for them, and re-layouts  3.8 us

profile of v5, /device:TPU:0, one launch (start us, length us, event | category | flops | bytes accessed | tf_op | source)
XLA Modules:
  0.0 115.3 jit_solution(9788981381124107260)
XLA Ops:
  0.6 1.8 %copy.38.refs_1_ = bf16[2,6,12,1024]{3,2,1,0:T(8,128)(2,1)} copy(bf16[2,6,12,1024]{3,0,2,1:T(2,128)(2,1)} %param.29) | data formatting | bytes 589824 | tf_op args[1]
  2.4 108.5 %shard_map.339 = (bf16[144,1024]{1,0:T(8,128)(2,1)}, bf16[576,512]{1,0:T(8,128)(2,1)}, f32[16,1152]{1,0:T(8,128)}, f32[16,1024]{1,0:T(8,128)}, f32[16,1024]{1,0:...) custom-call(bf16[576,512]{1,0:T(8,128)(2,1)} %bitcast.8, ...), custom_call_target="tpu_custom_call" | custom-call | tf_op jit(solution)/shard_map/pallas_call | solution.py:942
  111.0 2.3 %shard_map.340 = (bf16[2,6,12,1024]{3,2,1,0:T(8,128)(2,1)}, bf16[576,512]{1,0:T(8,128)(2,1)}, f32[1,4]{1,0:T(1,128)}, f32[4,1536]{1,0:T(4,128)}, f32[4,512]{1,0:...) custom-call(bf16[144,1024]{1,0:T(8,128)(2,1)} %get-tuple-element.28., ...), custom_call_target="tpu_custom_call" | custom-call | tf_op jit(solution)/shard_map/pallas_call | solution.py:1027
  113.3 2.0 %copy.39 = bf16[2,6,12,1024]{3,0,2,1:T(2,128)(2,1)} copy(bf16[2,6,12,1024]{3,2,1,0:T(8,128)(2,1)} %get-tuple-element.46) | data formatting | bytes 589824

commit v6 on v4

--- a/solution.py
+++ b/solution.py
@@ -278,8 +278,20 @@
             setattr(r, kind + matrix, getattr(r, held + matrix))
     r.patches_grad = r.fine_out
     r.normal, r.cot_flat, r.wide = r.tokens_back, r.coarse_attended, r.unit_coarse
+    r.back_packed, r.end_packed, r.out_packed = r.in_packed, r.mid_packed, r.cot_packed
     for name in LOADED[:6]:
         load(name)
+
+    for landed, size in (
+        (r.in_landed, 112),
+        (r.mid_landed, 112),
+        (r.back_landed, 112),
+        (r.end_landed, 112),
+        (r.cot_landed, 48),
+        (r.out_landed, 48),
+    ):
+        for start in PIECES[:2]:
+            landed[start + size : start + 128, :] = jnp.zeros((128 - size, landed.shape[1]), HALF)
 
     barrier = pltpu.get_barrier_semaphore()
     partners = [neighbour(step, way) for step in STEPS for way in (1, -1)] + [sibling]
@@ -304,6 +316,8 @@
 
     def gathered(kind, rows, value, sizes, needed):
         total = dot(getattr(r, kind + "_own")[rows, :], value)
+        if len(needed) == 3:
+            return total + dot(getattr(r, kind + "_halo")[rows, :], getattr(r, kind + "_landed")[...])
         for slot in needed:
             piece = slice(PIECES[slot], PIECES[slot] + sizes[slot])
             total = total + dot(getattr(r, kind + "_halo")[rows, piece], getattr(r, kind + "_landed")[piece, :])
@@ -323,16 +337,16 @@
         pack_piece("cot", cotangent, slot, coarse_sizes[slot])
     r.fine_out[...] = jnp.zeros_like(r.fine_out)
 
-    keep4, give4 = owner_pick(4, core), owner_pick(4, 1 - core)
-    keep8, give8 = owner_pick(8, core), owner_pick(8, 1 - core)
-    keep16, give16 = owner_pick(16, core), owner_pick(16, 1 - core)
-
-    def split(value, keep, give, name, rows):
+    pick4, pick8, pick16 = (
+        jnp.concatenate([owner_pick(n, core), owner_pick(n, 1 - core)], axis=1) for n in (4, 8, 16)
+    )
+
+    def split(value, pick, name, rows):
         for block in range(value.shape[1] // 256):
-            part = value[:, 256 * block : 256 * block + 256]
+            parts = dot(value[:, 256 * block : 256 * block + 256], pick).astype(HALF)
             cols = slice(128 * block, 128 * block + 128)
-            getattr(r, name + "_left")[rows, cols] = dot(part, keep).astype(HALF)
-            getattr(r, name + "_give")[rows, cols] = dot(part, give).astype(HALF)
+            getattr(r, name + "_left")[rows, cols] = parts[:, :128]
+            getattr(r, name + "_give")[rows, cols] = parts[:, 128:]
 
     def hand_left(name):
         count = getattr(r, name + "_give").shape[0]
@@ -384,10 +398,9 @@
             mid_arrive.append(send_piece("mid", slot, fine_sizes[slot], 1))
         if w == 2:
             cot_arrive = [send_piece("cot", n, coarse_sizes[n], 1) for n in (LAT, DIAG, LON)]
-    for w in range(4):
-        rows = slice(CELLS * w, CELLS * w + CELLS)
-        split(r.normal[rows, :], keep4, give4, "normal", rows)
-        split(r.attended[rows, :], keep4, give4, "attended", rows)
+    rows = slice(0, 576)
+    split(r.normal[...], pick4, "normal", rows)
+    split(r.attended[...], pick4, "attended", rows)
     handed_fine += [hand_left("normal"), hand_left("attended")]
     for name in LOADED[11:14]:
         load(name)
@@ -417,7 +430,7 @@
     merged = (unit * r.gain_m[...]).astype(HALF)
     loads["merge_w"].wait()
     coarse_in = dot(merged, r.merge_w[...]).astype(HALF).astype(FULL)
-    split(merged, keep16, give16, "merged", own)
+    split(merged, pick16, "merged", own)
     merged_handed = hand_left("merged")
     unit, scale_coarse = norm_parts(coarse_in)
     r.unit_coarse[...] = unit
@@ -426,7 +439,7 @@
     for n in range(3):
         cols = slice(1024 * n, 1024 * (n + 1))
         r.qkv_coarse[:, cols] = dot(normed, r.qkv_c[:, cols]).astype(HALF)
-    split(normed, keep8, give8, "normed", own)
+    split(normed, pick8, "normed", own)
     handed_coarse.append(hand_left("normed"))
     for copy in cot_arrive:
         copy.wait()
@@ -450,11 +463,11 @@
             r.qkv_right[own, 1024 * n + at : 1024 * n + at + 128] = grads[n]
     handed_coarse.append(hand_right("qkv_right", 0, CELLS))
     attended = r.coarse_attended[...]
-    split(attended, keep8, give8, "coarse", own)
+    split(attended, pick8, "coarse", own)
     handed_coarse.append(hand_left("coarse"))
     normed_grad = dot_nt(r.qkv_right[own, :], r.qkv_c[...]).astype(HALF).astype(FULL)
     gain_row = jnp.sum(normed_grad * r.unit_coarse[...], axis=0, keepdims=True)
-    split(in_two(gain_row), keep8, give8, "gain_coarse", slice(0, 16))
+    split(in_two(gain_row), pick8, "gain_coarse", slice(0, 16))
     gains_handed = [hand_left("gain_coarse")]
     coarse_grad = r.cot_right[own, :].astype(FULL) + norm_back(
         normed_grad, r.unit_coarse[...], scale_coarse, r.gain_c[...]
@@ -463,7 +476,7 @@
     inner_handed = hand_right("inner_right", 0, CELLS)
     merged_grad = dot_nt(r.inner_right[own, :], r.merge_w[...]).astype(HALF).astype(FULL)
     gain_row = jnp.sum(merged_grad * r.unit_merge[...], axis=0, keepdims=True)
-    split(in_two(gain_row), keep16, give16, "gain_merge", slice(0, 16))
+    split(in_two(gain_row), pick16, "gain_merge", slice(0, 16))
     gains_handed.append(hand_left("gain_merge"))
     back = norm_back(merged_grad, r.unit_merge[...], scale_merge, r.gain_m[...]).astype(HALF)
     for g in range(4):
@@ -526,7 +539,8 @@
                 landed[(0,) + at] = added(theirs[at], [landed[(0,) + at]]).astype(HALF)
                 return carry
 
-            lax.fori_loop(0, size // 2, add, 0, unroll=2)
+            for i in range(size // 2):
+                add(i, 0)
             sums[p][h, 2] = remote(landed.at[0, rows], landed.at[2, rows], there(axis, two))
 
     def collect(p, stage):
@@ -542,7 +556,8 @@
             landed[(1,) + at] = total.astype(HALF)
             return carry
 
-        lax.fori_loop(0, size, add, 0, unroll=4)
+        for i in range(size):
+            add(i, 0)
 
     def start_first(p):
         axis = ORDERS[p % 3][0]
@@ -569,7 +584,8 @@
             landed[(1,) + at] = total.astype(HALF)
             return carry
 
-        lax.fori_loop(0, size, add, 0, unroll=4)
+        for i in range(size):
+            add(i, 0)
 
     def start_second(p):
         source, landed, lead, size, axis = stage_of(p, 1)
@@ -732,7 +748,7 @@
             begin(0, 1)
             forward(1, 1)
             forward(2, 1)
-    split(in_two(gain_row), keep4, give4, "gain_fine", slice(0, 16))
+    split(in_two(gain_row), pick4, "gain_fine", slice(0, 16))
     gain_handed = hand_left("gain_fine")
     if summing:
         for p in (3, 4):
@@ -827,7 +843,8 @@
         operands.append(value)
     half = {name: values[name].shape for name in LOADED[:11]}
     for kind, width in (("in", 512), ("cot", 1024), ("mid", 512), ("back", 512), ("end", 512), ("out", 1024)):
-        half[kind + "_packed"] = half[kind + "_landed"] = (PACKED, width)
+        half[kind + "_landed"] = (PACKED, width)
+    half.update(in_packed=(PACKED, 512), cot_packed=(PACKED, 1024), mid_packed=(PACKED, 512))
     lefts = dict(
         normal=(576, 256),
         attended=(576, 256),

time: 102 us -> 101 us (level)
  Pallas kernels: 97.5 us -> 96.4 us
    pallas_call x1, Pallas kernels: 95.2 us -> 94.1 us  [whole(): pl.pallas_call(functools.partial(whole_kernel, names, summing), out_shape...]
where the time goes in v6:
time: 101 us
  Pallas kernels  96.4 us (95%)
  local copies, waits for them, and re-layouts  3.8 us (4%)
    pallas_call x1, Pallas kernels, whole(): pl.pallas_call(functools.partial(whole_kernel, names, summing), out_shape...  94.1 us
    unnamed x2, local copies, waits for them, and re-layouts  3.8 us
    pallas_call x1, Pallas kernels, last(): pl.pallas_call(last_kernel, out_shape=shapes, in_specs=[VMEM] * 8, out_sp...  2.3 us

profile of v6, /device:TPU:0, one launch (start us, length us, event | category | flops | bytes accessed | tf_op | source)
XLA Modules:
  0.0 100.8 jit_solution(15896619907189248696)
XLA Ops:
  0.6 1.8 %copy.38.refs_1_ = bf16[2,6,12,1024]{3,2,1,0:T(8,128)(2,1)} copy(bf16[2,6,12,1024]{3,0,2,1:T(2,128)(2,1)} %param.29) | data formatting | bytes 589824 | tf_op args[1]
  2.4 94.1 %shard_map.339 = (bf16[144,1024]{1,0:T(8,128)(2,1)}, bf16[576,512]{1,0:T(8,128)(2,1)}, f32[16,1152]{1,0:T(8,128)}, f32[16,1024]{1,0:T(8,128)}, f32[16,1024]{1,0:...) custom-call(bf16[576,512]{1,0:T(8,128)(2,1)} %bitcast.8, ...), custom_call_target="tpu_custom_call" | custom-call | tf_op jit(solution)/shard_map/pallas_call | solution.py:902
  96.5 2.3 %shard_map.340 = (bf16[2,6,12,1024]{3,2,1,0:T(8,128)(2,1)}, bf16[576,512]{1,0:T(8,128)(2,1)}, f32[1,4]{1,0:T(1,128)}, f32[4,1536]{1,0:T(4,128)}, f32[4,512]{1,0:...) custom-call(bf16[144,1024]{1,0:T(8,128)(2,1)} %get-tuple-element.28., ...), custom_call_target="tpu_custom_call" | custom-call | tf_op jit(solution)/shard_map/pallas_call | solution.py:987
  98.8 2.0 %copy.39 = bf16[2,6,12,1024]{3,0,2,1:T(2,128)(2,1)} copy(bf16[2,6,12,1024]{3,2,1,0:T(8,128)(2,1)} %get-tuple-element.46) | data formatting | bytes 589824

commit v7 on v6

--- a/solution.py
+++ b/solution.py
@@ -493,14 +493,6 @@
 
     sums = {}
 
-    def across(axis):
-        mine = place[axis]
-        near, far = mine + 1 - 2 * (mine % 2), 3 - mine
-        return mine, ((near, far), (far, near))
-
-    def there(axis, index):
-        return device_at({**place, axis: index}, core)
-
     def stage_of(p, stage):
         landed = of(r, ("landed0_", "landed1_")[stage], p)
         lead = LEADS[p % 3][stage]
@@ -510,54 +502,6 @@
         else:
             source = lambda index: second_cut(p % 3, of(r, "landed0_", p).at[1], index)
         return source, landed, lead, size, ORDERS[p % 3][stage]
-
-    def halves(lead):
-        return [pl.ds(h * (lead[0] // 2), lead[0] // 2) for h in range(2)]
-
-    def begin(p, stage):
-        source, landed, lead, size, axis = stage_of(p, stage)
-        mine, pairs = across(axis)
-        sums[p] = {}
-        for slot in range(2):
-            for h, rows in enumerate(halves(lead)):
-                one = pairs[h][0]
-                quarter = lax.rem(mine + 2, 4) if slot == 0 else one
-                sums[p][h, slot] = remote(
-                    source(quarter).at[rows], landed.at[slot, rows], there(axis, one)
-                )
-
-    def forward(p, stage):
-        source, landed, lead, size, axis = stage_of(p, stage)
-        mine, pairs = across(axis)
-        for h, rows in enumerate(halves(lead)):
-            two = pairs[h][1]
-            theirs = source(two)
-            sums[p][h, 0].wait()
-
-            def add(i, carry, h=h, theirs=theirs):
-                at = spots(lead, i + h * (size // 2))
-                landed[(0,) + at] = added(theirs[at], [landed[(0,) + at]]).astype(HALF)
-                return carry
-
-            for i in range(size // 2):
-                add(i, 0)
-            sums[p][h, 2] = remote(landed.at[0, rows], landed.at[2, rows], there(axis, two))
-
-    def collect(p, stage):
-        source, landed, lead, size, axis = stage_of(p, stage)
-        mine = source(place[axis])
-        for h in range(2):
-            sums[p][h, 1].wait()
-            sums[p][h, 2].wait()
-
-        def add(i, carry):
-            at = spots(lead, i)
-            total = added(mine[at], [landed[(1,) + at], landed[(2,) + at]])
-            landed[(1,) + at] = total.astype(HALF)
-            return carry
-
-        for i in range(size):
-            add(i, 0)
 
     def start_first(p):
         axis = ORDERS[p % 3][0]
@@ -652,8 +596,8 @@
 
     lax.fori_loop(0, 2, qkv_rows, 0)
     if summing:
-        begin(1, 0)
-        begin(2, 0)
+        start_first(1)
+        start_first(2)
     for copy in gains_handed + [merged_handed, inner_handed]:
         copy.wait()
     ones = jnp.ones((32, 128), HALF)
@@ -672,7 +616,7 @@
 
     lax.fori_loop(0, 4, merge_rows, 0)
     if summing:
-        begin(0, 0)
+        start_first(0)
 
     needs = ((LON, LAT, DIAG), (LAT,), (LON,), ())
     waited = set()
@@ -700,9 +644,6 @@
         handed_fine.append(hand_right("triple_right", CELLS * w, CELLS))
         if w == 3:
             out_arrive = [send_piece("out", n, coarse_sizes[n], -1) for n in (LAT, DIAG, LON)]
-        if summing:
-            for p in {2: (1, 2), 0: (0,)}.get(w, ()):
-                forward(p, 0)
     for copy in handed_fine:
         copy.wait()
 
@@ -726,9 +667,6 @@
     if summing:
         for p in (3, 4):
             start_first(p)
-        for p in (1, 2):
-            collect(p, 0)
-            begin(p, 1)
     gain_row = jnp.zeros((1, 512), FULL)
     r.tokens_back[...] = jnp.zeros_like(r.tokens_back)
     for w in (3, 2, 1, 0):
@@ -743,40 +681,32 @@
                 loads["end_pack"].wait()
             pack_piece("end", r.tokens_back[...], slot, fine_sizes[slot])
             end_arrive.append(send_piece("end", slot, fine_sizes[slot], -1))
-        if summing and w == 2:
-            collect(0, 0)
-            begin(0, 1)
-            forward(1, 1)
-            forward(2, 1)
     split(in_two(gain_row), pick4, "gain_fine", slice(0, 16))
     gain_handed = hand_left("gain_fine")
     if summing:
-        for p in (3, 4):
+        for p in (1, 2):
             collect_first(p)
             start_second(p)
-        forward(0, 1)
     gain_handed.wait()
     for n in range(2):
         cols = slice(128 * n, 128 * n + 128)
         store(n, 5, 0, [dot_tn(r.gain_fine_left[:, cols], ones)] * 4)
     if summing:
         start_first(5)
+        for p in (0, 3, 4):
+            collect_first(p)
+            start_second(p)
     for copy in out_arrive:
         copy.wait()
     r.coarse_tokens[...] = gathered(
         "out", every, r.coarse_out[...], coarse_sizes, (LON, LAT, DIAG)
     ).astype(HALF)
     if summing:
-        for p in (1, 2):
-            collect(p, 1)
-            start_third(p)
         collect_first(5)
         start_second(5)
-        for p in (3, 4):
+        for p in (1, 2, 0, 3, 4):
             collect_second(p)
             start_third(p)
-        collect(0, 1)
-        start_third(0)
     for name in ("end_own", "end_halo"):
         loads[name].wait()
     for copy in end_arrive:

time: 101 us -> 102 us (level)
  Pallas kernels: 96.4 us -> 97.5 us
    pallas_call x1, Pallas kernels: 94.1 us -> 95.2 us  [whole(): pl.pallas_call(functools.partial(whole_kernel, names, summing), out_shape...]
where the time goes in v7:
time: 102 us
  Pallas kernels  97.5 us (96%)
  local copies, waits for them, and re-layouts  3.8 us (4%)
    pallas_call x1, Pallas kernels, whole(): pl.pallas_call(functools.partial(whole_kernel, names, summing), out_shape...  95.2 us
    unnamed x2, local copies, waits for them, and re-layouts  3.8 us
    pallas_call x1, Pallas kernels, last(): pl.pallas_call(last_kernel, out_shape=shapes, in_specs=[VMEM] * 8, out_sp...  2.3 us

profile of v7, /device:TPU:0, one launch (start us, length us, event | category | flops | bytes accessed | tf_op | source)
XLA Modules:
  0.0 101.9 jit_solution(11360480729138394986)
XLA Ops:
  0.6 1.8 %copy.38.refs_1_ = bf16[2,6,12,1024]{3,2,1,0:T(8,128)(2,1)} copy(bf16[2,6,12,1024]{3,0,2,1:T(2,128)(2,1)} %param.29) | data formatting | bytes 589824 | tf_op args[1]
  2.4 95.2 %shard_map.339 = (bf16[144,1024]{1,0:T(8,128)(2,1)}, bf16[576,512]{1,0:T(8,128)(2,1)}, f32[16,1152]{1,0:T(8,128)}, f32[16,1024]{1,0:T(8,128)}, f32[16,1024]{1,0:...) custom-call(bf16[576,512]{1,0:T(8,128)(2,1)} %bitcast.8, ...), custom_call_target="tpu_custom_call" | custom-call | tf_op jit(solution)/shard_map/pallas_call | solution.py:832
  97.6 2.3 %shard_map.340 = (bf16[2,6,12,1024]{3,2,1,0:T(8,128)(2,1)}, bf16[576,512]{1,0:T(8,128)(2,1)}, f32[1,4]{1,0:T(1,128)}, f32[4,1536]{1,0:T(4,128)}, f32[4,512]{1,0:...) custom-call(bf16[144,1024]{1,0:T(8,128)(2,1)} %get-tuple-element.28., ...), custom_call_target="tpu_custom_call" | custom-call | tf_op jit(solution)/shard_map/pallas_call | solution.py:917
  99.9 2.0 %copy.39 = bf16[2,6,12,1024]{3,0,2,1:T(2,128)(2,1)} copy(bf16[2,6,12,1024]{3,2,1,0:T(8,128)(2,1)} %get-tuple-element.46) | data formatting | bytes 589824

commit v8 on v6

--- a/solution.py
+++ b/solution.py
@@ -129,24 +129,29 @@
 
 
 def pair_weights(queries, keys, mask):
-    scores = dot_nt(keys, queries * 0.125)
-    scores = jnp.where(mask, MASKED, scores)
-    powers = jnp.exp(scores - jnp.max(scores, axis=0, keepdims=True))
-    return powers * (1.0 / jnp.sum(powers, axis=0, keepdims=True))
+    scores = [dot_nt(key, query * 0.125) for query, key in zip(queries, keys)]
+    scores = [jnp.where(mask, MASKED, score) for score in scores]
+    powers = [jnp.exp(score - jnp.max(score, axis=0, keepdims=True)) for score in scores]
+    return [power * (1.0 / jnp.sum(power, axis=0, keepdims=True)) for power in powers]
 
 
 def pair_forward(rounded, values):
-    return one_pair(dot_tn(rounded, values)).astype(HALF)
+    stacks = [dot_tn(weights, value) for weights, value in zip(rounded, values)]
+    return [one_pair(stack).astype(HALF) for stack in stacks]
 
 
 def pair_back(weights, rounded, queries, keys, values, upstream):
-    weight_grad = dot_nt(values, upstream)
-    inner = jnp.sum(weights * weight_grad, axis=0, keepdims=True)
-    score_grad = (weights * (weight_grad - inner) * 0.125).astype(HALF)
-    query_grad = one_pair(dot_tn(score_grad, keys)).astype(HALF)
-    key_grad = dot(score_grad, queries).astype(HALF)
-    value_grad = dot(rounded, upstream).astype(HALF)
-    return query_grad, key_grad, value_grad
+    weight_grads = [dot_nt(value, above) for value, above in zip(values, upstream)]
+    value_grads = [dot(half, above).astype(HALF) for half, above in zip(rounded, upstream)]
+    score_grads = []
+    for weight, grad in zip(weights, weight_grads):
+        inner = jnp.sum(weight * grad, axis=0, keepdims=True)
+        score_grads.append((weight * (grad - inner) * 0.125).astype(HALF))
+    key_grads = [dot(grad, query).astype(HALF) for grad, query in zip(score_grads, queries)]
+    query_grads = [
+        one_pair(dot_tn(grad, key)).astype(HALF) for grad, key in zip(score_grads, keys)
+    ]
+    return query_grads, key_grads, value_grads
 
 
 def four_stacked(pieces):
@@ -382,15 +387,17 @@
             cols = slice(512 * n, 512 * n + 512)
             qkv[rows, cols] = dot(normed, r.qkv_f[:, cols]).astype(HALF)
         mask = pair_mask(edge if w >= 2 else 0)
+        lanes = [slice(128 * p, 128 * p + 128) for p in range(4)]
+
+        def parts(base):
+            return [qkv[rows, base + 128 * p : base + 128 * p + 128] for p in range(4)]
+
+        weights = pair_weights([two_heads(part) for part in parts(0)], parts(512), mask)
+        rounded = [weight.astype(HALF) for weight in weights]
+        for p, mixed in enumerate(pair_forward(rounded, parts(1024))):
+            r.attended[rows, lanes[p]] = mixed
         for p in range(4):
-            at = 128 * p
-            queries = two_heads(qkv[rows, at : at + 128])
-            weights = pair_weights(queries, qkv[rows, 512 + at : 640 + at], mask)
-            rounded = weights.astype(HALF)
-            r.kept[4 * w + p] = rounded
-            r.attended[rows, at : at + 128] = pair_forward(
-                rounded, qkv[rows, 1024 + at : 1152 + at]
-            )
+            r.kept[4 * w + p] = rounded[p]
         attended = r.attended[rows, :]
         r.fine_out[rows, :] = (values + dot(attended, r.proj_f[...])).astype(HALF)
         for slot in {1: (LAT,), 2: (DIAG, LON)}.get(w, ()):
@@ -450,17 +457,23 @@
     r.cot_attended[...] = dot_nt(cot, r.proj_c[...]).astype(HALF)
     qkv = r.qkv_coarse
     mask = pair_mask(edge)
-    for p in range(8):
-        at = 128 * p
-        queries = two_heads(qkv[:, at : at + 128])
-        keys, worth = qkv[:, 1024 + at : 1152 + at], qkv[:, 2048 + at : 2176 + at]
+    for group in range(2):
+        starts = [512 * group + 128 * p for p in range(4)]
+
+        def parts(base, held=qkv, starts=starts):
+            return [held[:, base + at : base + at + 128] for at in starts]
+
+        queries = [two_heads(part) for part in parts(0)]
+        keys, worth = parts(1024), parts(2048)
         weights = pair_weights(queries, keys, mask)
-        rounded = weights.astype(HALF)
-        r.coarse_attended[:, at : at + 128] = pair_forward(rounded, worth)
-        upstream = two_heads(r.cot_attended[:, at : at + 128])
+        rounded = [weight.astype(HALF) for weight in weights]
+        for at, mixed in zip(starts, pair_forward(rounded, worth)):
+            r.coarse_attended[:, at : at + 128] = mixed
+        upstream = [two_heads(part) for part in parts(0, r.cot_attended)]
         grads = pair_back(weights, rounded, queries, keys, worth, upstream)
         for n in range(3):
-            r.qkv_right[own, 1024 * n + at : 1024 * n + at + 128] = grads[n]
+            for at, grad in zip(starts, grads[n]):
+                r.qkv_right[own, 1024 * n + at : 1024 * n + at + 128] = grad
     handed_coarse.append(hand_right("qkv_right", 0, CELLS))
     attended = r.coarse_attended[...]
     split(attended, pick8, "coarse", own)
@@ -688,15 +701,24 @@
         handed_fine.append(hand_right("fine_right", CELLS * w, CELLS))
         attended_grad = dot_nt(grad, r.proj_f[...]).astype(HALF)
         qkv = r.qkv
-        for p in range(4):
-            at = 128 * p
-            queries = two_heads(qkv[rows, at : at + 128])
-            keys, worth = qkv[rows, 512 + at : 640 + at], qkv[rows, 1024 + at : 1152 + at]
-            rounded = r.kept[4 * w + p]
-            upstream = two_heads(attended_grad[:, at : at + 128])
-            grads = pair_back(rounded.astype(FULL), rounded, queries, keys, worth, upstream)
-            for n in range(3):
-                r.triple_right[rows, 512 * n + at : 512 * n + at + 128] = grads[n]
+
+        def parts(base):
+            return [qkv[rows, base + 128 * p : base + 128 * p + 128] for p in range(4)]
+
+        rounded = [r.kept[4 * w + p] for p in range(4)]
+        upstream = [two_heads(attended_grad[:, 128 * p : 128 * p + 128]) for p in range(4)]
+        grads = pair_back(
+            [half.astype(FULL) for half in rounded],
+            rounded,
+            [two_heads(part) for part in parts(0)],
+            parts(512),
+            parts(1024),
+            upstream,
+        )
+        for n in range(3):
+            for p in range(4):
+                at = 512 * n + 128 * p
+                r.triple_right[rows, at : at + 128] = grads[n][p]
         handed_fine.append(hand_right("triple_right", CELLS * w, CELLS))
         if w == 3:
             out_arrive = [send_piece("out", n, coarse_sizes[n], -1) for n in (LAT, DIAG, LON)]

time: 101 us -> 99.7 us (0.987)
  Pallas kernels: 96.4 us -> 95 us
    pallas_call x1, Pallas kernels: 94.1 us -> 92.7 us  [whole(): pl.pallas_call(functools.partial(whole_kernel, names, summing), out_shape...]
where the time goes in v8:
time: 99.7 us; the launch traced here: 99.4 us
  Pallas kernels  95 us (95%)
  local copies, waits for them, and re-layouts  3.8 us (4%)
    pallas_call x1, Pallas kernels, whole(): pl.pallas_call(functools.partial(whole_kernel, names, summing), out_shape...  92.7 us
    unnamed x2, local copies, waits for them, and re-layouts  3.8 us
    pallas_call x1, Pallas kernels, last(): pl.pallas_call(last_kernel, out_shape=shapes, in_specs=[VMEM] * 8, out_sp...  2.3 us

profile of v8, /device:TPU:0, one launch (start us, length us, event | category | flops | bytes accessed | tf_op | source)
XLA Modules:
  0.0 99.4 jit_solution(10395684143453214368)
XLA Ops:
  0.6 1.8 %copy.38.refs_1_ = bf16[2,6,12,1024]{3,2,1,0:T(8,128)(2,1)} copy(bf16[2,6,12,1024]{3,0,2,1:T(2,128)(2,1)} %param.29) | data formatting | bytes 589824 | tf_op args[1]
  2.4 92.7 %shard_map.339 = (bf16[144,1024]{1,0:T(8,128)(2,1)}, bf16[576,512]{1,0:T(8,128)(2,1)}, f32[16,1152]{1,0:T(8,128)}, f32[16,1024]{1,0:T(8,128)}, f32[16,1024]{1,0:...) custom-call(bf16[576,512]{1,0:T(8,128)(2,1)} %bitcast.8, ...), custom_call_target="tpu_custom_call" | custom-call | tf_op jit(solution)/shard_map/pallas_call | solution.py:924
  95.1 2.3 %shard_map.340 = (bf16[2,6,12,1024]{3,2,1,0:T(8,128)(2,1)}, bf16[576,512]{1,0:T(8,128)(2,1)}, f32[1,4]{1,0:T(1,128)}, f32[4,1536]{1,0:T(4,128)}, f32[4,512]{1,0:...) custom-call(bf16[144,1024]{1,0:T(8,128)(2,1)} %get-tuple-element.28., ...), custom_call_target="tpu_custom_call" | custom-call | tf_op jit(solution)/shard_map/pallas_call | solution.py:1009
  97.4 2.0 %copy.39 = bf16[2,6,12,1024]{3,0,2,1:T(2,128)(2,1)} copy(bf16[2,6,12,1024]{3,2,1,0:T(8,128)(2,1)} %get-tuple-element.46) | data formatting | bytes 589824
